TPU v7x, 32 devices: a whole 2x2x4 slice. The times are simulated.
32 devices in a mesh: groups: 2 (over y), seq: 16 (over z, x, core).
Axes of the slice: x: 2, y: 2, z: 4, core: 2. Of those that a mesh axis runs over, the one named last changes fastest.
Arguments:
- queries: bfloat16 [8192, 2048], P(('groups', 'seq')), parts along dimension 0, may hold values from -128 to 128
- keys: bfloat16 [32768, 1024], P(('groups', 'seq')), parts along dimension 0, may hold values from -6 to 6
- values: bfloat16 [32768, 1024], P(('groups', 'seq')), parts along dimension 0, may hold values from -6 to 6
- dirty: int32 [32], P(('groups', 'seq')), parts along dimension 0, may hold values from -1 to 3
- spans: int32 [32, 2], P(('groups', 'seq')), parts along dimension 0, may hold values from 0 to 16384, as said below
Outputs:
- attended: bfloat16 [8192, 2048], P(('groups', 'seq')), parts along dimension 0
There are 2 independent parts, one for each index of `groups`. A program takes and returns all parts, laid end to end along the dimension named above; each array names one. Nothing has to cross between parts.
Inputs may be any that keep to these rules, and one draw needn't show every extreme that they name: -1 marks a shard with no dirty block. `spans`: row k holds the start and the exclusive end of the one tombstoned span of shard k: k * 1024 <= start < end <= (k + 1) * 1024, with end - start from 1 to 32; the last shard's span has exactly 32 rows.
All inputs are finite; a program needn't handle non-finite values.
Results may differ from a plain program's by a relative error of at most 0.014.
Values may be sent and summed in bfloat16 or wider, within the bound.
A program may use at most 128 MiB of HBM per device.

v0:
```python
import math

import jax
import jax.numpy as jnp
from jax import lax
from jax.sharding import PartitionSpec as P

HEAD_DIMENSION = 128
WINDOW = 4096
BLOCK_ROWS = 256


softcap_limit = 50.0
query_scale = 144.0 ** (-0.5)


def from_behind(array, axis, by):
    count = lax.axis_size(axis)
    pairs = [(i, i + by) for i in range(count) if 0 <= i + by < count]
    return lax.ppermute(array, axis, pairs)


def locate(raw, spans):
    begin = spans[:, 0]
    finish = spans[:, 1]
    offset = raw[:, None] - begin[None, :]
    before = jnp.sum(jnp.clip(offset, 0, (finish - begin)[None, :]), axis=1)
    inside = jnp.sum(
        ((raw[:, None] >= begin[None, :]) & (raw[:, None] < finish[None, :])).astype(jnp.int32),
        axis=1,
    )
    return (raw - before, (inside == 0) & (raw >= 0))


def apply_rotary(field, place):
    half = field.shape[-1] // 2
    order = jnp.arange(half, dtype=jnp.float32)
    freq = jnp.exp(order * (-2.0 * math.log(10000.0) / field.shape[-1]))
    angle = place[:, None] * freq[None, :]
    cosine = jnp.cos(angle)[:, None, :]
    sine = jnp.sin(angle)[:, None, :]
    first = field[..., :half]
    second = field[..., half:]
    return jnp.concatenate(
        [first * cosine - second * sine, second * cosine + first * sine], axis=-1
    )


def attend(query_block, query_raw, query_pos, window_k, window_v, key_raw, key_pos, key_live):
    count = window_k.shape[0]
    kv_heads = window_k.shape[1] // HEAD_DIMENSION
    head_group = query_block.shape[2]
    tile = math.gcd(512, count)
    turns = count // tile
    items = (
        window_k.reshape(turns, tile, kv_heads, HEAD_DIMENSION),
        window_v.reshape(turns, tile, kv_heads, HEAD_DIMENSION),
        key_raw.reshape(turns, tile),
        key_pos.reshape(turns, tile),
        key_live.reshape(turns, tile),
    )

    def visit(carry, item):
        numerator, total = carry
        tile_k, tile_v, tile_raw, tile_pos, tile_live = item
        score = jnp.einsum(
            "qhgd,khd->hgqk", query_block, tile_k, preferred_element_type=jnp.float32
        )
        capped = softcap_limit * jnp.tanh(score / softcap_limit)
        allowed = (
            tile_live[None, :]
            & (tile_raw[None, :] <= query_raw[:, None])
            & (query_pos[:, None] - tile_pos[None, :] < WINDOW)
        )
        weight = jnp.where(allowed[None, None], jnp.exp(capped), jnp.float32(0.0))
        total = total + jnp.sum(weight, axis=-1)
        numerator = numerator + jnp.einsum(
            "nexi,inv->xnev",
            weight.astype(jnp.bfloat16),
            tile_v,
            preferred_element_type=jnp.float32,
        )
        return ((numerator, total), None)

    rows_q = query_block.shape[0]
    start_numer = jnp.zeros((rows_q, kv_heads, head_group, HEAD_DIMENSION), jnp.float32)
    start_total = jnp.zeros((kv_heads, head_group, rows_q), jnp.float32)
    (numerator, total), unused = lax.scan(visit, (start_numer, start_total), items)
    return (numerator, total)


def body(queries, keys, values, dirty, spans):
    every_span, every_dirty = (
        lax.all_gather(spans, "seq", axis=0, tiled=True),
        lax.all_gather(dirty, "seq", axis=0, tiled=True),
    )
    shard_index = lax.axis_index("seq")
    rows = keys.shape[0]
    columns = keys.shape[1]
    kv_heads = columns // HEAD_DIMENSION
    q_heads = queries.shape[1] // HEAD_DIMENSION
    head_group = q_heads // kv_heads
    back = WINDOW // rows + 1
    own_raw = shard_index * rows + jnp.arange(rows)
    own_pos, own_live = locate(own_raw, every_span)
    key_rot = apply_rotary(
        keys.astype(jnp.float32).reshape(rows, kv_heads, HEAD_DIMENSION),
        own_pos.astype(jnp.float32),
    )
    key_rot = key_rot.astype(jnp.bfloat16).reshape(rows, columns)
    block = every_dirty[shard_index]
    chosen = jnp.maximum(block, 0)
    q_raw = shard_index * rows + chosen * BLOCK_ROWS + jnp.arange(BLOCK_ROWS)
    q_pos, q_live = locate(q_raw, every_span)
    query_rotary = (
        apply_rotary(
            queries.astype(jnp.float32).reshape(BLOCK_ROWS, q_heads, HEAD_DIMENSION),
            q_pos.astype(jnp.float32),
        )
        * query_scale
    )
    query_rotary = query_rotary.astype(jnp.bfloat16).reshape(
        BLOCK_ROWS, kv_heads, head_group, HEAD_DIMENSION
    )
    numerator, total = attend(
        query_rotary, q_raw, q_pos, key_rot, values, own_raw, own_pos, own_live
    )
    last = lax.axis_size("seq") - 1
    for step in range(1, back + 1):
        visitor = from_behind(query_rotary, "seq", -step)
        asking = jnp.minimum(shard_index + step, last)
        asking_block = jnp.maximum(every_dirty[asking], 0)
        asking_raw = asking * rows + asking_block * BLOCK_ROWS + jnp.arange(BLOCK_ROWS)
        asking_pos, unused_live = locate(asking_raw, every_span)
        part_numer, part_total = attend(
            visitor, asking_raw, asking_pos, key_rot, values, own_raw, own_pos, own_live
        )
        back_numer, back_total = from_behind((part_numer, part_total), "seq", step)
        numerator = numerator + back_numer
        total = total + back_total
    total = jnp.where(total > 0, total, jnp.float32(1.0))
    result = numerator / jnp.transpose(total, (2, 0, 1))[..., None]
    keep = q_live & (block >= 0)
    result = jnp.where(keep[:, None, None, None], result, jnp.float32(0.0))
    return result.reshape(BLOCK_ROWS, q_heads * HEAD_DIMENSION).astype(jnp.bfloat16)


def solution(mesh):
    placed = (
        P(("groups", "seq"), None),
        P(("groups", "seq"), None),
        P(("groups", "seq"), None),
        P(("groups", "seq")),
        P(("groups", "seq"), None),
    )
    return jax.shard_map(
        body, mesh=mesh, in_specs=placed, out_specs=P(("groups", "seq"), None), check_vma=False
    )
```

profile of v0, /device:TPU:28, one launch (start us, length us, event | category | flops | bytes accessed | tf_op | source)
XLA Modules:
  0.0 487.0 jit_solution(8376926354485233773)
XLA Ops:
  0.0 16.8 %all-gather = s32[16,1,2]{2,1,0:T(1,128)S(1)} all-gather(s32[1,1,2]{2,1,0:T(1,128)} %bitcast.319), channel_id=1, replica_groups=mesh['groups'=2,'seq'=16] {'seq'}, dimensions={0}, use_global_device_ids=true | all-gather | bytes 136 | tf_op jit(solution)/shard_map/all_gather | solution.py:94
  19.6 13.1 %all-reduce = s32[16]{0:T(128)S(1)} all-reduce(s32[16]{0:T(128)S(1)} %dynamic-update-slice), channel_id=1, replica_groups=mesh['groups'=2,'seq'=16] {'seq'}, use_global_device_ids=true, to_apply=%add | all-reduce | flops 16 | bytes 128
  79.3 32.4 %while.79 = (s32[]{:T(128)}, f32[256,8,2,128]{0,3,2,1:T(8,128)}, f32[8,2,256]{2,1,0:T(2,128)}, bf16[2,512,8,128]{1,3,2,0:T(8,128)(2,1)}, pred[2,512]{1,0:T(4,128...) while((s32[]{:T(128)}, f32[256,8,2,128]{0,3,2,1:T(8,128)}, ...), condition=%wide.region_10.11_spmd.clone, body=%wide.region_8.10_spmd.clone.sunk | while | flops 1092227328 | bytes 32982192 | solution.py:88
  79.7 7.3 %fusion.179 = (f32[8,2,256]{2,1,0:T(2,128)S(1)}, f32[8,512,256,2]{2,1,3,0:T(8,128)}) fusion(pred[256,512]{0,1:T(8,128)(4,1)S(1)} %fusion.178, bf16[256,8,2,128]{3,0,2,1:T(8,128)(2,1)} %get-tuple-element.1670, bf16[2,512,8,128]{3,1,2,0:T(8,128)(2,1)} %get-tuple-element.1669, s32[]{:T(128)} %get-tuple-element.1648), kind=kOutput, calls=%fused_computation.30.clone.1 | convolution fusion | flops 545255424 | bytes 10633728 | tf_op jit(solution)/shard_map/while/body/eval_jaxpr/qhgd,khd->hgqk/dot_general | solution.py:66
  95.2 7.3 %fusion.179 = (f32[8,2,256]{2,1,0:T(2,128)S(1)}, f32[8,512,256,2]{2,1,3,0:T(8,128)}) fusion(pred[256,512]{0,1:T(8,128)(4,1)S(1)} %fusion.178, bf16[256,8,2,128]{3,0,2,1:T(8,128)(2,1)} %get-tuple-element.1670, bf16[2,512,8,128]{3,1,2,0:T(8,128)(2,1)} %get-tuple-element.1669, s32[]{:T(128)} %get-tuple-element.1648), kind=kOutput, calls=%fused_computation.30.clone.1 | convolution fusion | flops 545255424 | bytes 10633728 | tf_op jit(solution)/shard_map/while/body/eval_jaxpr/qhgd,khd->hgqk/dot_general | solution.py:66
  102.5 7.9 %bitcast_add_fusion.13 = f32[256,8,2,128]{0,3,2,1:T(8,128)} fusion(f32[256,8,2,128]{0,3,2,1:T(8,128)} %get-tuple-element.1649, f32[8,512,256,2]{2,1,3,0:T(8,128)} %get-tuple-element.1378, pred[256,512]{0,1:T(8,128)(4,1)S(1)} %fusion.178, bf16[2,512,8,128]{1,3,2,0:T(8,128)(2,1)S(1)} %copy-done.1, s32[]{:T(128)} %get-tuple-element.1648, pred[]{:T(512)S(6)} %compare.19), kind=kOutput, calls=%fused_computation.34.clone.1 | convolution fusion | flops 546308096 | bytes 13762565 | tf_op jit(solution)/shard_map/while/body/eval_jaxpr/nexi,inv->xnev/dot_general | solution.py:77
  114.3 30.7 %while.80 = (s32[]{:T(128)}, f32[256,8,2,128]{0,3,2,1:T(8,128)}, f32[8,2,256]{2,1,0:T(2,128)S(1)}, bf16[2,512,8,128]{1,3,2,0:T(8,128)(2,1)}, pred[2,512]{1,0:T(4...) while((s32[]{:T(128)}, f32[256,8,2,128]{0,3,2,1:T(8,128)}, ...), condition=%wide.region_14.15_spmd.clone, body=%wide.region_12.14_spmd.clone.sunk | while | flops 1092227328 | bytes 32982192 | solution.py:88
  137.2 7.9 %bitcast_add_fusion.14 = f32[256,8,2,128]{0,3,2,1:T(8,128)} fusion(f32[256,8,2,128]{0,3,2,1:T(8,128)} %get-tuple-element.1571, f32[8,512,256,2]{2,1,3,0:T(8,128)} %get-tuple-element.1393, pred[256,512]{0,1:T(8,128)(4,1)S(1)} %fusion.183, bf16[2,512,8,128]{1,3,2,0:T(8,128)(2,1)S(1)} %copy-done.2, s32[]{:T(128)} %get-tuple-element.1570, pred[]{:T(512)S(6)} %compare.20), kind=kOutput, calls=%fused_computation.57.clone.1 | convolution fusion | flops 546308096 | bytes 13762565 | tf_op jit(solution)/shard_map/while/body/eval_jaxpr/nexi,inv->xnev/dot_general | solution.py:77
  148.3 30.6 %while.81 = (s32[]{:T(128)}, f32[256,8,2,128]{0,3,2,1:T(8,128)}, f32[8,2,256]{2,1,0:T(2,128)S(1)}, bf16[2,512,8,128]{1,3,2,0:T(8,128)(2,1)}, pred[2,512]{1,0:T(4...) while((s32[]{:T(128)}, f32[256,8,2,128]{0,3,2,1:T(8,128)}, ...), condition=%wide.region_18.19_spmd.clone, body=%wide.region_16.18_spmd.clone.sunk | while | flops 1092227328 | bytes 32982192 | solution.py:88
  148.7 7.3 %fusion.189 = (f32[8,2,256]{2,1,0:T(2,128)S(1)}, f32[8,512,256,2]{2,1,3,0:T(8,128)}) fusion(pred[256,512]{0,1:T(8,128)(4,1)S(1)} %fusion.188, bf16[256,8,2,128]{3,0,2,1:T(8,128)(2,1)} %get-tuple-element.1553, bf16[2,512,8,128]{3,1,2,0:T(8,128)(2,1)} %get-tuple-element.1552, s32[]{:T(128)} %get-tuple-element.1531), kind=kOutput, calls=%fused_computation.76.clone.1 | convolution fusion | flops 545255424 | bytes 10633728 | tf_op jit(solution)/shard_map/while/body/eval_jaxpr/qhgd,khd->hgqk/dot_general | solution.py:66
  156.0 7.3 %bitcast_add_fusion.15 = f32[256,8,2,128]{0,3,2,1:T(8,128)} fusion(f32[256,8,2,128]{0,3,2,1:T(8,128)} %get-tuple-element.1532, f32[8,512,256,2]{2,1,3,0:T(8,128)} %get-tuple-element.1408, pred[256,512]{0,1:T(8,128)(4,1)S(1)} %fusion.188, bf16[2,512,8,128]{1,3,2,0:T(8,128)(2,1)S(1)} %copy-done.3, s32[]{:T(128)} %get-tuple-element.1531, pred[]{:T(512)S(6)} %compare.21), kind=kOutput, calls=%fused_computation.80.clone.1 | convolution fusion | flops 546308096 | bytes 13762565 | tf_op jit(solution)/shard_map/while/body/eval_jaxpr/nexi,inv->xnev/dot_general | solution.py:77
  163.7 7.3 %fusion.189 = (f32[8,2,256]{2,1,0:T(2,128)S(1)}, f32[8,512,256,2]{2,1,3,0:T(8,128)}) fusion(pred[256,512]{0,1:T(8,128)(4,1)S(1)} %fusion.188, bf16[256,8,2,128]{3,0,2,1:T(8,128)(2,1)} %get-tuple-element.1553, bf16[2,512,8,128]{3,1,2,0:T(8,128)(2,1)} %get-tuple-element.1552, s32[]{:T(128)} %get-tuple-element.1531), kind=kOutput, calls=%fused_computation.76.clone.1 | convolution fusion | flops 545255424 | bytes 10633728 | tf_op jit(solution)/shard_map/while/body/eval_jaxpr/qhgd,khd->hgqk/dot_general | solution.py:66
  171.0 7.9 %bitcast_add_fusion.15 = f32[256,8,2,128]{0,3,2,1:T(8,128)} fusion(f32[256,8,2,128]{0,3,2,1:T(8,128)} %get-tuple-element.1532, f32[8,512,256,2]{2,1,3,0:T(8,128)} %get-tuple-element.1408, pred[256,512]{0,1:T(8,128)(4,1)S(1)} %fusion.188, bf16[2,512,8,128]{1,3,2,0:T(8,128)(2,1)S(1)} %copy-done.3, s32[]{:T(128)} %get-tuple-element.1531, pred[]{:T(512)S(6)} %compare.21), kind=kOutput, calls=%fused_computation.80.clone.1 | convolution fusion | flops 546308096 | bytes 13762565 | tf_op jit(solution)/shard_map/while/body/eval_jaxpr/nexi,inv->xnev/dot_general | solution.py:77
  180.9 31.0 %while.82 = (s32[]{:T(128)}, f32[256,8,2,128]{0,3,2,1:T(8,128)}, f32[8,2,256]{2,1,0:T(2,128)S(1)}, bf16[2,512,8,128]{1,3,2,0:T(8,128)(2,1)}, pred[2,512]{1,0:T(4...) while((s32[]{:T(128)}, f32[256,8,2,128]{0,3,2,1:T(8,128)}, ...), condition=%wide.region_22.23_spmd.clone, body=%wide.region_20.22_spmd.clone.sunk | while | flops 1092227328 | bytes 32982192 | solution.py:88
  181.7 7.3 %fusion.194 = (f32[8,2,256]{2,1,0:T(2,128)S(1)}, f32[8,512,256,2]{2,1,3,0:T(8,128)}) fusion(pred[256,512]{0,1:T(8,128)(4,1)S(1)} %fusion.193, bf16[256,8,2,128]{3,0,2,1:T(8,128)(2,1)} %get-tuple-element.1514, bf16[2,512,8,128]{3,1,2,0:T(8,128)(2,1)} %get-tuple-element.1513, s32[]{:T(128)} %get-tuple-element.1492), kind=kOutput, calls=%fused_computation.99.clone.1 | convolution fusion | flops 545255424 | bytes 10633728 | tf_op jit(solution)/shard_map/while/body/eval_jaxpr/qhgd,khd->hgqk/dot_general | solution.py:66
  204.0 7.9 %bitcast_add_fusion.16 = f32[256,8,2,128]{0,3,2,1:T(8,128)} fusion(f32[256,8,2,128]{0,3,2,1:T(8,128)} %get-tuple-element.1493, f32[8,512,256,2]{2,1,3,0:T(8,128)} %get-tuple-element.1423, pred[256,512]{0,1:T(8,128)(4,1)S(1)} %fusion.193, bf16[2,512,8,128]{1,3,2,0:T(8,128)(2,1)S(1)} %copy-done.4, s32[]{:T(128)} %get-tuple-element.1492, pred[]{:T(512)S(6)} %compare.22), kind=kOutput, calls=%fused_computation.103.clone.1 | convolution fusion | flops 546308096 | bytes 13762565 | tf_op jit(solution)/shard_map/while/body/eval_jaxpr/nexi,inv->xnev/dot_general | solution.py:77
  213.2 30.6 %while.83 = (s32[]{:T(128)}, f32[256,8,2,128]{0,3,2,1:T(8,128)}, f32[8,2,256]{2,1,0:T(2,128)S(1)}, bf16[2,512,8,128]{1,3,2,0:T(8,128)(2,1)}, pred[2,512]{1,0:T(4...) while((s32[]{:T(128)}, f32[256,8,2,128]{0,3,2,1:T(8,128)}, ...), condition=%wide.region_26.27_spmd.clone, body=%wide.region_24.26_spmd.clone.sunk | while | flops 1092227328 | bytes 32982192 | solution.py:88
  220.9 7.3 %bitcast_add_fusion.17 = f32[256,8,2,128]{0,3,2,1:T(8,128)} fusion(f32[256,8,2,128]{0,3,2,1:T(8,128)} %get-tuple-element.1454, f32[8,512,256,2]{2,1,3,0:T(8,128)} %get-tuple-element.1438, pred[256,512]{0,1:T(8,128)(4,1)S(1)} %fusion.198, bf16[2,512,8,128]{1,3,2,0:T(8,128)(2,1)S(1)} %copy-done.5, s32[]{:T(128)} %get-tuple-element.1453, pred[]{:T(512)S(6)} %compare.23), kind=kOutput, calls=%fused_computation.126.clone.1 | convolution fusion | flops 546308096 | bytes 13762565 | tf_op jit(solution)/shard_map/while/body/eval_jaxpr/nexi,inv->xnev/dot_general | solution.py:77
  235.9 7.9 %bitcast_add_fusion.17 = f32[256,8,2,128]{0,3,2,1:T(8,128)} fusion(f32[256,8,2,128]{0,3,2,1:T(8,128)} %get-tuple-element.1454, f32[8,512,256,2]{2,1,3,0:T(8,128)} %get-tuple-element.1438, pred[256,512]{0,1:T(8,128)(4,1)S(1)} %fusion.198, bf16[2,512,8,128]{1,3,2,0:T(8,128)(2,1)S(1)} %copy-done.5, s32[]{:T(128)} %get-tuple-element.1453, pred[]{:T(512)S(6)} %compare.23), kind=kOutput, calls=%fused_computation.126.clone.1 | convolution fusion | flops 546308096 | bytes 13762565 | tf_op jit(solution)/shard_map/while/body/eval_jaxpr/nexi,inv->xnev/dot_general | solution.py:77
  253.7 30.7 %while.78 = (s32[]{:T(128)}, f32[256,8,2,128]{0,3,2,1:T(8,128)}, f32[8,2,256]{2,1,0:T(2,128)S(1)}, bf16[2,512,8,128]{1,3,2,0:T(8,128)(2,1)}, pred[2,512]{1,0:T(4...) while((s32[]{:T(128)}, f32[256,8,2,128]{0,3,2,1:T(8,128)}, ...), condition=%wide.region_6.7_spmd.clone, body=%wide.region_4.6_spmd.clone.sunk | while | flops 1092227328 | bytes 32982192 | solution.py:88
  276.5 7.9 %bitcast_add_fusion.12 = f32[256,8,2,128]{0,3,2,1:T(8,128)} fusion(f32[256,8,2,128]{0,3,2,1:T(8,128)} %get-tuple-element.1610, f32[8,512,256,2]{2,1,3,0:T(8,128)} %get-tuple-element.1363, pred[256,512]{0,1:T(8,128)(4,1)S(1)} %fusion.173, bf16[2,512,8,128]{1,3,2,0:T(8,128)(2,1)S(1)} %copy-done.6, s32[]{:T(128)} %get-tuple-element.1609, pred[]{:T(512)S(6)} %compare.18), kind=kOutput, calls=%fused_computation.11.clone.1 | convolution fusion | flops 546308096 | bytes 13762565 | tf_op jit(solution)/shard_map/while/body/eval_jaxpr/nexi,inv->xnev/dot_general | solution.py:77
  285.8 7.4 %collective-permute-done.1 = f32[256,8,2,128]{0,3,2,1:T(8,128)} collective-permute-done((f32[256,8,2,128]{0,3,2,1:T(8,128)}, f32[256,8,2,128]{0,3,2,1:T(8,128)}, u32[]{:S(2)}, u32[]{:S(2)}) %collective-permute-start.1) | collective-permute-done | bytes 2097184 | tf_op jit(solution)/shard_map/ppermute | solution.py:20
  299.6 37.6 %collective-permute-done.5 = f32[256,8,2,128]{0,3,2,1:T(8,128)} collective-permute-done((f32[256,8,2,128]{0,3,2,1:T(8,128)}, f32[256,8,2,128]{0,3,2,1:T(8,128)}, u32[]{:S(2)}, u32[]{:S(2)}) %collective-permute-start.5) | collective-permute-done | bytes 2097184 | tf_op jit(solution)/shard_map/ppermute | solution.py:20
  337.2 142.2 %collective-permute-done.9 = f32[256,8,2,128]{0,3,2,1:T(8,128)} collective-permute-done((f32[256,8,2,128]{0,3,2,1:T(8,128)}, f32[256,8,2,128]{0,3,2,1:T(8,128)}, u32[]{:S(2)}, u32[]{:S(2)}) %collective-permute-start.9) | collective-permute-done | bytes 2097184 | tf_op jit(solution)/shard_map/ppermute | solution.py:20
  (189 shorter events, 164.1 us)
Async XLA Ops:
  42.7 14.7 %copy-start = (bf16[1024,1024]{1,0:T(8,128)(2,1)S(1)}, bf16[1024,1024]{1,0:T(8,128)(2,1)}, u32[]{:S(2)}) copy-start(bf16[1024,1024]{1,0:T(8,128)(2,1)} %param.18) | copy-start | bytes 6291460
  44.3 35.0 %collective-permute-start = (bf16[256,8,2,128]{3,0,2,1:T(8,128)(2,1)}, bf16[256,8,2,128]{3,0,2,1:T(8,128)(2,1)}, u32[]{:S(2)}, u32[]{:S(2)}) collective-permute-start(bf16[256,8,2,128]{3,0,2,1:T(8,128)(2,1)} %fusion.120), channel_id=1, source_target_pairs={{1,0},{2,1},{3,2},{4,3},{5,4},{6,5},{7,6},{8,7},{9,8},{10,9},{11,1... | collective-permute-start | bytes 3145736 | tf_op jit(solution)/shard_map/ppermute | solution.py:20
  46.2 68.1 %collective-permute-start.2 = (bf16[256,8,2,128]{3,0,2,1:T(8,128)(2,1)}, bf16[256,8,2,128]{3,0,2,1:T(8,128)(2,1)}, u32[]{:S(2)}, u32[]{:S(2)}) collective-permute-start(bf16[256,8,2,128]{3,0,2,1:T(8,128)(2,1)} %fusion.120), channel_id=1, source_target_pairs={{2,0},{3,1},{4,2},{5,3},{6,4},{7,5},{8,6},{9,7},{10,8},{11,9},{12,... | collective-permute-start | bytes 3145736 | tf_op jit(solution)/shard_map/ppermute | solution.py:20
  48.2 100.2 %collective-permute-start.4 = (bf16[256,8,2,128]{3,0,2,1:T(8,128)(2,1)}, bf16[256,8,2,128]{3,0,2,1:T(8,128)(2,1)}, u32[]{:S(2)}, u32[]{:S(2)}) collective-permute-start(bf16[256,8,2,128]{3,0,2,1:T(8,128)(2,1)} %fusion.120), channel_id=1, source_target_pairs={{3,0},{4,1},{5,2},{6,3},{7,4},{8,5},{9,6},{10,7},{11,8},{12,9},{13... | collective-permute-start | bytes 3145736 | tf_op jit(solution)/shard_map/ppermute | solution.py:20
  50.8 130.1 %collective-permute-start.6 = (bf16[256,8,2,128]{3,0,2,1:T(8,128)(2,1)}, bf16[256,8,2,128]{3,0,2,1:T(8,128)(2,1)}, u32[]{:S(2)}, u32[]{:S(2)}) collective-permute-start(bf16[256,8,2,128]{3,0,2,1:T(8,128)(2,1)} %fusion.120), channel_id=1, source_target_pairs={{4,0},{5,1},{6,2},{7,3},{8,4},{9,5},{10,6},{11,7},{12,8},{13,9},{1... | collective-permute-start | bytes 3145736 | tf_op jit(solution)/shard_map/ppermute | solution.py:20
  53.9 159.3 %collective-permute-start.8 = (bf16[256,8,2,128]{3,0,2,1:T(8,128)(2,1)}, bf16[256,8,2,128]{3,0,2,1:T(8,128)(2,1)}, u32[]{:S(2)}, u32[]{:S(2)}) collective-permute-start(bf16[256,8,2,128]{3,0,2,1:T(8,128)(2,1)} %fusion.120), channel_id=1, source_target_pairs={{5,0},{6,1},{7,2},{8,3},{9,4},{10,5},{11,6},{12,7},{13,8},{14,9},{... | collective-permute-start | bytes 3145736 | tf_op jit(solution)/shard_map/ppermute | solution.py:20
  79.6 7.3 %copy-start.1 = (bf16[2,512,8,128]{1,3,2,0:T(8,128)(2,1)S(1)}, bf16[2,512,8,128]{1,3,2,0:T(8,128)(2,1)}, u32[]{:S(2)}) copy-start(bf16[2,512,8,128]{1,3,2,0:T(8,128)(2,1)} %get-tuple-element.1664) | copy-start | bytes 6291460 | tf_op jit(solution)/shard_map/while
  111.7 133.5 %collective-permute-start.10 = (f32[8,2,256]{2,1,0:T(2,128)}, f32[8,2,256]{2,1,0:T(2,128)}, u32[]{:S(2)}, u32[]{:S(2)}) collective-permute-start(f32[8,2,256]{2,1,0:T(2,128)} %get-tuple-element.360), channel_id=1, source_target_pairs={{0,1},{1,2},{2,3},{3,4},{4,5},{5,6},{6,7},{7,8},{8,9},{9,10},{10,1... | collective-permute-start | bytes 49160 | tf_op jit(solution)/shard_map/ppermute | solution.py:20
  145.0 102.1 %collective-permute-start.11 = (f32[8,2,256]{2,1,0:T(2,128)S(1)}, f32[8,2,256]{2,1,0:T(2,128)S(1)}, u32[]{:S(2)}, u32[]{:S(2)}) collective-permute-start(f32[8,2,256]{2,1,0:T(2,128)S(1)} %get-tuple-element.361), channel_id=1, source_target_pairs={{0,2},{1,3},{2,4},{3,5},{4,6},{5,7},{6,8},{7,9},{8,10},{9,11},{10,... | collective-permute-start | bytes 49160 | tf_op jit(solution)/shard_map/ppermute | solution.py:20
  148.7 7.3 %copy-start.3 = (bf16[2,512,8,128]{1,3,2,0:T(8,128)(2,1)S(1)}, bf16[2,512,8,128]{1,3,2,0:T(8,128)(2,1)}, u32[]{:S(2)}) copy-start(bf16[2,512,8,128]{1,3,2,0:T(8,128)(2,1)} %get-tuple-element.1547) | copy-start | bytes 6291460 | tf_op jit(solution)/shard_map/while
  163.7 7.3 %copy-start.3 = (bf16[2,512,8,128]{1,3,2,0:T(8,128)(2,1)S(1)}, bf16[2,512,8,128]{1,3,2,0:T(8,128)(2,1)}, u32[]{:S(2)}) copy-start(bf16[2,512,8,128]{1,3,2,0:T(8,128)(2,1)} %get-tuple-element.1547) | copy-start | bytes 6291460 | tf_op jit(solution)/shard_map/while
  179.0 70.1 %collective-permute-start.12 = (f32[8,2,256]{2,1,0:T(2,128)S(1)}, f32[8,2,256]{2,1,0:T(2,128)S(1)}, u32[]{:S(2)}, u32[]{:S(2)}) collective-permute-start(f32[8,2,256]{2,1,0:T(2,128)S(1)} %get-tuple-element.362), channel_id=1, source_target_pairs={{0,3},{1,4},{2,5},{3,6},{4,7},{5,8},{6,9},{7,10},{8,11},{9,12},{10... | collective-permute-start | bytes 49160 | tf_op jit(solution)/shard_map/ppermute | solution.py:20
  180.9 32.3 %copy-start.7 = (f32[8,2,256]{2,1,0:T(2,128)S(1)}, f32[8,2,256]{2,1,0:T(2,128)}, u32[]{:S(2)}) copy-start(f32[8,2,256]{2,1,0:T(2,128)} %custom-call.11) | copy-start | bytes 49156
  180.9 32.3 %copy-start.9 = (s32[256]{0:T(256)S(1)}, s32[256]{0:T(256)}, u32[]{:S(2)}) copy-start(s32[256]{0:T(256)} %fusion.128) | copy-start | bytes 3076
  181.7 7.3 %copy-start.4 = (bf16[2,512,8,128]{1,3,2,0:T(8,128)(2,1)S(1)}, bf16[2,512,8,128]{1,3,2,0:T(8,128)(2,1)}, u32[]{:S(2)}) copy-start(bf16[2,512,8,128]{1,3,2,0:T(8,128)(2,1)} %get-tuple-element.1508) | copy-start | bytes 6291460 | tf_op jit(solution)/shard_map/while
  211.9 39.1 %collective-permute-start.13 = (f32[8,2,256]{2,1,0:T(2,128)S(1)}, f32[8,2,256]{2,1,0:T(2,128)S(1)}, u32[]{:S(2)}, u32[]{:S(2)}) collective-permute-start(f32[8,2,256]{2,1,0:T(2,128)S(1)} %get-tuple-element.363), channel_id=1, source_target_pairs={{0,4},{1,5},{2,6},{3,7},{4,8},{5,9},{6,10},{7,11},{8,12},{9,13},{1... | collective-permute-start | bytes 49160 | tf_op jit(solution)/shard_map/ppermute | solution.py:20
  213.2 40.4 %copy-start.8 = (s32[256]{0:T(256)S(1)}, s32[256]{0:T(256)}, u32[]{:S(2)}) copy-start(s32[256]{0:T(256)} %get-tuple-element.1602) | copy-start | bytes 3076
  243.9 8.5 %collective-permute-start.14 = (f32[8,2,256]{2,1,0:T(2,128)S(1)}, f32[8,2,256]{2,1,0:T(2,128)S(1)}, u32[]{:S(2)}, u32[]{:S(2)}) collective-permute-start(f32[8,2,256]{2,1,0:T(2,128)S(1)} %get-tuple-element.364), channel_id=1, source_target_pairs={{0,5},{1,6},{2,7},{3,8},{4,9},{5,10},{6,11},{7,12},{8,13},{9,14},{... | collective-permute-start | bytes 49160 | tf_op jit(solution)/shard_map/ppermute | solution.py:20
  245.2 48.0 %collective-permute-start.1 = (f32[256,8,2,128]{0,3,2,1:T(8,128)}, f32[256,8,2,128]{0,3,2,1:T(8,128)}, u32[]{:S(2)}, u32[]{:S(2)}) collective-permute-start(f32[256,8,2,128]{0,3,2,1:T(8,128)} %get-tuple-element.354), channel_id=1, source_target_pairs={{0,1},{1,2},{2,3},{3,4},{4,5},{5,6},{6,7},{7,8},{8,9},{9,10},{10,1... | collective-permute-start | bytes 6291464 | tf_op jit(solution)/shard_map/ppermute | solution.py:20
  247.2 52.4 %collective-permute-start.3 = (f32[256,8,2,128]{0,3,2,1:T(8,128)}, f32[256,8,2,128]{0,3,2,1:T(8,128)}, u32[]{:S(2)}, u32[]{:S(2)}) collective-permute-start(f32[256,8,2,128]{0,3,2,1:T(8,128)} %get-tuple-element.355), channel_id=1, source_target_pairs={{0,2},{1,3},{2,4},{3,5},{4,6},{5,7},{6,8},{7,9},{8,10},{9,11},{10,... | collective-permute-start | bytes 6291464 | tf_op jit(solution)/shard_map/ppermute | solution.py:20
  249.1 88.1 %collective-permute-start.5 = (f32[256,8,2,128]{0,3,2,1:T(8,128)}, f32[256,8,2,128]{0,3,2,1:T(8,128)}, u32[]{:S(2)}, u32[]{:S(2)}) collective-permute-start(f32[256,8,2,128]{0,3,2,1:T(8,128)} %get-tuple-element.356), channel_id=1, source_target_pairs={{0,3},{1,4},{2,5},{3,6},{4,7},{5,8},{6,9},{7,10},{8,11},{9,12},{10... | collective-permute-start | bytes 6291464 | tf_op jit(solution)/shard_map/ppermute | solution.py:20
  251.0 86.1 %collective-permute-start.7 = (f32[256,8,2,128]{0,3,2,1:T(8,128)}, f32[256,8,2,128]{0,3,2,1:T(8,128)}, u32[]{:S(2)}, u32[]{:S(2)}) collective-permute-start(f32[256,8,2,128]{0,3,2,1:T(8,128)} %get-tuple-element.357), channel_id=1, source_target_pairs={{0,4},{1,5},{2,6},{3,7},{4,8},{5,9},{6,10},{7,11},{8,12},{9,13},{1... | collective-permute-start | bytes 6291464 | tf_op jit(solution)/shard_map/ppermute | solution.py:20
  252.3 227.1 %collective-permute-start.9 = (f32[256,8,2,128]{0,3,2,1:T(8,128)}, f32[256,8,2,128]{0,3,2,1:T(8,128)}, u32[]{:S(2)}, u32[]{:S(2)}) collective-permute-start(f32[256,8,2,128]{0,3,2,1:T(8,128)} %get-tuple-element.358), channel_id=1, source_target_pairs={{0,5},{1,6},{2,7},{3,8},{4,9},{5,10},{6,11},{7,12},{8,13},{9,14},{... | collective-permute-start | bytes 6291464 | tf_op jit(solution)/shard_map/ppermute | solution.py:20
  253.7 31.4 %copy-start.10 = (s32[256]{0:T(256)S(1)}, s32[256]{0:T(256)}, u32[]{:S(2)}) copy-start(s32[256]{0:T(256)} %get-tuple-element.799) | copy-start | bytes 3076
  (8 other events, 58.5 us)
where the time goes:
time: 493 us; the launch traced here: 487 us
  waiting for transfers between devices  194 us (39%)
  matrix products  179 us (36%)
  starting transfers between devices  30.5 us (6%)
  blocking collectives  29.9 us (6%)
  other arithmetic  26.7 us (5%)
  local copies, waits for them, and re-layouts  20.1 us (4%)
  between operations  5.9 us (1%)
    ppermute x15, waiting for transfers between devices, from_behind(): return lax.ppermute(array, axis, pairs)  194 us
    dot_general x12, matrix products, visit(): jnp.einsum('nexi,inv->xnev', weight.astype(jnp.bfloat16), tile_v, preferr...  91.1 us
    dot_general x12, matrix products, visit(): jnp.einsum('qhgd,khd->hgqk', query_block, tile_k, preferred_element_type=...  87.7 us
    ppermute x15, starting transfers between devices, from_behind(): return lax.ppermute(array, axis, pairs)  30.5 us
    all_gather x1, blocking collectives, body(): lax.all_gather(spans, 'seq', axis=0, tiled=True)  16.8 us
    unnamed x1, blocking collectives  13.1 us
    unnamed x17, local copies, waits for them, and re-layouts  11.2 us
  transfers between devices with their start and end apart: 15, of which 4 were waited for; matrix products, arithmetic and copies ran while one was open for 43% of the time, Pallas kernels for 0%

commit v1 on v0

v1 whole, which is shorter than its diff:
```python
import functools
import math

import jax
import jax.numpy as jnp
from jax import lax
from jax.experimental import pallas as pl
from jax.experimental.pallas import tpu as pltpu
from jax.sharding import PartitionSpec as P

HEAD = 128
WINDOW = 4096
BLOCK = 256
CAP = 50.0
QUERY_SCALE = 144.0 ** (-0.5)
LOG2E = math.log2(math.e)
VMEM = pl.BlockSpec(memory_space=pltpu.VMEM)
SMEM = pl.BlockSpec(memory_space=pltpu.SMEM)
PARAMS = pltpu.CompilerParams(vmem_limit_bytes=48 * 1024 * 1024)


def removed_before(meta, shard):
    def add(s, total):
        return total + meta[3 * s + 2] - meta[3 * s + 1]

    return lax.fori_loop(0, shard, add, jnp.int32(0))


def tables(row, base, begin, length):
    lane = lax.broadcasted_iota(jnp.int32, row.shape, 1)
    order = (lane % (HEAD // 2)).astype(jnp.float32)
    freq = jnp.exp(order * (-2.0 * math.log(10000.0) / HEAD))
    place = row - base - jnp.clip(row - begin, 0, length)
    angle = place.astype(jnp.float32) * freq
    low = lane < HEAD // 2
    cosine, sine = jnp.cos(angle), jnp.sin(angle)
    cosine_swap = pltpu.roll(cosine, HEAD // 2, 1)
    sine_swap = pltpu.roll(sine, HEAD // 2, 1)
    return (
        (jnp.where(low, cosine, cosine_swap), jnp.where(low, -sine, sine_swap)),
        (jnp.where(low, cosine_swap, cosine), jnp.where(low, -sine_swap, sine)),
    )


def rotate(x, table):
    x = x.astype(jnp.float32)
    return x * table[0] + pltpu.roll(x, HEAD // 2, 1) * table[1]


def rope_q_kernel(meta, mine, other, out):
    me = lax.axis_index("seq")
    core = me % 2
    rows_shard = 1024
    half = BLOCK // 2
    for which, ref in enumerate((mine, other)):
        slot = core if which == 0 else 1 - core
        shard = me - core + slot
        block = jnp.maximum(meta[3 * shard], 0)
        begin = meta[3 * shard + 1]
        length = meta[3 * shard + 2] - begin
        base = removed_before(meta, shard)
        raw0 = shard * rows_shard + block * BLOCK
        tile = 32

        @pl.loop(0, half // tile)
        def _(step):
            at = pl.multiple_of(step * tile, tile)
            row = lax.broadcasted_iota(jnp.int32, (tile, HEAD), 0) + raw0 + at
            lane = lax.broadcasted_iota(jnp.int32, (tile, HEAD), 1)
            row = row + jnp.where(lane < HEAD // 2, 0, half)
            both = tables(row, base, begin, length)
            for part in range(2):
                src = pl.multiple_of(at + part * half, tile)
                dst = pl.multiple_of(slot * BLOCK + src, tile)
                for h in range(out.shape[1] // HEAD):
                    cols = pl.ds(h * HEAD, HEAD)
                    x = rotate(ref[pl.ds(src, tile), cols], both[part]) * QUERY_SCALE
                    out[pl.ds(dst, tile), cols] = x.astype(jnp.bfloat16)


def prep_kv_kernel(meta, k_mine, k_other, v_mine, v_other, k_out, v_out, live_out):
    me = lax.axis_index("seq")
    core = me % 2
    rows = k_mine.shape[0]
    half = rows // 2
    for which, (k_ref, v_ref) in enumerate(((k_mine, v_mine), (k_other, v_other))):
        slot = core if which == 0 else 1 - core
        shard = me - core + slot
        begin = meta[3 * shard + 1]
        finish = meta[3 * shard + 2]
        base = removed_before(meta, shard)
        raw0 = shard * rows
        tile = 32

        @pl.loop(0, half // tile)
        def _(step):
            at = pl.multiple_of(step * tile, tile)
            iota = lax.broadcasted_iota(jnp.int32, (tile, HEAD), 0)
            lane = lax.broadcasted_iota(jnp.int32, (tile, HEAD), 1)
            row = iota + raw0 + at + jnp.where(lane < HEAD // 2, 0, half)
            both = tables(row, base, begin, finish - begin)
            for part in range(2):
                src = pl.multiple_of(at + part * half, tile)
                dst = pl.multiple_of(slot * rows + src, tile)
                raw = iota + raw0 + src
                live = jnp.where((raw >= begin) & (raw < finish), 0.0, 1.0)
                live_out[pl.ds(dst, tile), :] = live.astype(jnp.bfloat16)
                for h in range(k_out.shape[1] // HEAD):
                    cols = pl.ds(h * HEAD, HEAD)
                    x = rotate(k_ref[pl.ds(src, tile), cols], both[part])
                    k_out[pl.ds(dst, tile), cols] = x.astype(jnp.bfloat16)
                    y = v_ref[pl.ds(src, tile), cols].astype(jnp.float32) * live
                    v_out[pl.ds(dst, tile), cols] = y.astype(jnp.bfloat16)


def visit(meta, q_ref, k_ref, v_ref, live_ref, acc, at, slot, mask):
    kv_heads = k_ref.shape[1] // HEAD
    rows = pl.ds(pl.multiple_of(at, BLOCK), BLOCK)
    q_rows = pl.ds(pl.multiple_of(slot * BLOCK, BLOCK), BLOCK)

    def scores(h):
        q = jnp.concatenate(
            [q_ref[q_rows, pl.ds((2 * h + g) * HEAD, HEAD)] for g in range(2)], axis=0
        )
        k = k_ref[rows, pl.ds(h * HEAD, HEAD)]
        return lax.dot_general(
            q, k, (((1,), (1,)), ((), ())), preferred_element_type=jnp.float32
        )

    s = scores(0)
    for h in range(kv_heads):
        ahead = scores(h + 1) if h + 1 < kv_heads else None
        weight = jnp.exp2(jnp.tanh(s * (1.0 / CAP)) * (CAP * LOG2E))
        if mask is not None:
            weight = jnp.where(mask, weight, 0.0)
        v = jnp.concatenate([v_ref[rows, pl.ds(h * HEAD, HEAD)], live_ref[rows, :]], axis=1)
        acc[h] += jnp.dot(weight.astype(jnp.bfloat16), v, preferred_element_type=jnp.float32)
        s = ahead


def allowed(meta, shard_q, raw_q, shard_k, raw_k):
    column = lax.broadcasted_iota(jnp.int32, (2 * BLOCK, 1), 0)
    q = raw_q + jnp.where(column < BLOCK, column, column - BLOCK)
    k = raw_k + lax.broadcasted_iota(jnp.int32, (1, BLOCK), 1)
    begin_q, end_q = meta[3 * shard_q + 1], meta[3 * shard_q + 2]
    begin_k, end_k = meta[3 * shard_k + 1], meta[3 * shard_k + 2]
    between = removed_before(meta, shard_q) - removed_before(meta, shard_k)
    q_place = q - between - jnp.clip(q - begin_q, 0, end_q - begin_q)
    k_place = k - jnp.clip(k - begin_k, 0, end_k - begin_k)
    return (k <= q) & (q_place - k_place < WINDOW)


def attend_kernel(away, n, tail, meta, q_ref, k_ref, v_ref, live_ref, *rest):
    if tail:
        tail_k, tail_v, tail_live, out, acc = rest
    else:
        out, acc = rest
    me = lax.axis_index("seq")
    chip = me // 2
    rows = k_ref.shape[0] // 2
    per_shard = rows // BLOCK
    count = 2 * per_shard
    first = chip * count
    kv_heads = k_ref.shape[1] // HEAD
    reach = WINDOW // BLOCK

    @pl.loop(0, 2)
    def _(slot):
        wanted = 2 * (chip + away) + slot
        shard = jnp.minimum(wanted, n - 1)
        block = meta[3 * shard]
        on = (wanted < n) & (block >= 0)
        block = jnp.maximum(block, 0)
        g = shard * per_shard + block - first
        lo = jnp.clip(g - reach - 1, 0, count)
        full_lo = jnp.clip(g - reach + 1, 0, count)
        full_hi = jnp.clip(g, 0, count)
        hi = jnp.clip(g + 1, 0, count)
        raw_q = (first + g) * BLOCK
        acc[...] = jnp.zeros_like(acc)

        @pl.loop(full_lo, jnp.where(on, full_hi, full_lo))
        def _(j):
            visit(meta, q_ref, k_ref, v_ref, live_ref, acc, j * BLOCK, slot, None)

        front = full_lo - lo

        @pl.loop(0, jnp.where(on, front + hi - full_hi, 0))
        def _(i):
            j = jnp.where(i < front, lo + i, full_hi + i - front)
            shard_k = 2 * chip + j // per_shard
            mask = allowed(meta, shard, raw_q, shard_k, (first + j) * BLOCK)
            visit(meta, q_ref, k_ref, v_ref, live_ref, acc, j * BLOCK, slot, mask)

        if tail:
            raw_k = (first + g - reach - 1) * BLOCK

            @pl.when(on & (g == 0) & (raw_k >= 0))
            def _():
                shard_k = jnp.maximum((first + g - reach - 1) // per_shard, 0)
                mask = allowed(meta, shard, raw_q, shard_k, raw_k)
                visit(meta, q_ref, tail_k, tail_v, tail_live, acc, 0, slot, mask)

        to = pl.ds(pl.multiple_of(slot * BLOCK, BLOCK), BLOCK)
        lane = lax.broadcasted_iota(jnp.int32, (BLOCK, HEAD), 1)
        packed = jnp.zeros((BLOCK, HEAD), jnp.float32)
        for h in range(kv_heads):
            for part in range(2):
                head = 2 * h + part
                mine = pl.ds(part * BLOCK, BLOCK)
                out[to, pl.ds(head * HEAD, HEAD)] = acc[h, mine, pl.ds(0, HEAD)].astype(
                    jnp.bfloat16
                )
                total = acc[h, mine, pl.ds(HEAD, HEAD)]
                coarse = total.astype(jnp.bfloat16).astype(jnp.float32)
                packed = jnp.where(lane == head, coarse, packed)
                packed = jnp.where(lane == head + 2 * kv_heads, total - coarse, packed)
        out[to, pl.ds(2 * kv_heads * HEAD, HEAD)] = packed.astype(jnp.bfloat16)


def finish_kernel(meta, *refs):
    parts, out = refs[:-1], refs[-1]
    me = lax.axis_index("seq")
    heads = out.shape[1] // HEAD
    per = BLOCK

    @pl.loop(0, 2)
    def _(slot):
        shard = me - me % 2 + slot
        block = meta[3 * shard]
        begin, end = meta[3 * shard + 1], meta[3 * shard + 2]
        raw0 = shard * 1024 + jnp.maximum(block, 0) * BLOCK
        rows = pl.ds(pl.multiple_of(slot * per, per), per)
        raw = raw0 + lax.broadcasted_iota(jnp.int32, (per, HEAD), 0)
        gone = (raw >= begin) & (raw < end)
        keep = jnp.logical_not(gone) & (block >= 0)
        totals = jnp.zeros((per, HEAD), jnp.float32)
        for part in parts:
            totals += part[rows, pl.ds(heads * HEAD, HEAD)].astype(jnp.float32)
        for h in range(heads):
            cols = pl.ds(h * HEAD, HEAD)
            total = totals[:, h : h + 1] + totals[:, heads + h : heads + h + 1]
            total = jnp.broadcast_to(jnp.where(total > 0, total, 1.0), (per, HEAD))
            value = jnp.zeros((per, HEAD), jnp.float32)
            for part in parts:
                value += part[rows, cols].astype(jnp.float32)
            value = jnp.where(keep, value / total, 0.0)
            out[rows, cols] = value.astype(jnp.bfloat16)


def call(kernel, inputs, shapes, scratch=(), cost=None):
    return pl.pallas_call(
        kernel,
        out_shape=shapes,
        in_specs=[SMEM] + [VMEM] * (len(inputs) - 1),
        out_specs=jax.tree.map(lambda _: VMEM, shapes),
        scratch_shapes=list(scratch),
        compiler_params=PARAMS,
        cost_estimate=cost,
    )(*inputs)


def shift(array, by, n):
    pairs = [(i, i + by) for i in range(n) if 0 <= i + by < n]
    return lax.ppermute(array, "seq", pairs)


def flip(array, n):
    return lax.ppermute(array, "seq", [(i, i ^ 1) for i in range(n)])


def half_of(array, which):
    width = array.shape[1] // 2
    return lax.dynamic_slice_in_dim(array, which * width, width, axis=1)


def body(queries, keys, values, dirty, spans):
    n = lax.axis_size("seq")
    core = lax.axis_index("seq") % 2
    bf = jnp.bfloat16
    own = jnp.concatenate([dirty[:, None], spans], axis=1)
    meta = lax.all_gather(own, "seq", axis=0, tiled=True).reshape(-1)
    q_other = flip(half_of(queries, 1 - core), n)
    k_other = flip(half_of(keys, 1 - core), n)
    v_other = flip(half_of(values, 1 - core), n)
    q_mine, k_mine, v_mine = (half_of(a, core) for a in (queries, keys, values))
    rows, width = k_mine.shape
    q = call(
        rope_q_kernel,
        (meta, q_mine, q_other),
        jax.ShapeDtypeStruct((2 * BLOCK, q_mine.shape[1]), bf),
        cost=pl.CostEstimate(flops=10**7, bytes_accessed=2**21, transcendentals=0),
    )
    visitors = [shift(q, -2 * d, n) for d in (1, 2)]
    k, v, live = call(
        prep_kv_kernel,
        (meta, k_mine, k_other, v_mine, v_other),
        (
            jax.ShapeDtypeStruct((2 * rows, width), bf),
            jax.ShapeDtypeStruct((2 * rows, width), bf),
            jax.ShapeDtypeStruct((2 * rows, HEAD), bf),
        ),
        cost=pl.CostEstimate(flops=10**8, bytes_accessed=2**23, transcendentals=0),
    )
    last = jnp.concatenate([k[-BLOCK:], v[-BLOCK:], live[-BLOCK:]], axis=1)
    last = shift(last, 6, n)
    tail = (last[:, :width], last[:, width : 2 * width], last[:, 2 * width :])
    shape = jax.ShapeDtypeStruct((2 * BLOCK, q.shape[1] + HEAD), bf)
    scratch = [pltpu.VMEM((width // HEAD, 2 * BLOCK, 2 * HEAD), jnp.float32)]
    cost = pl.CostEstimate(flops=6 * 10**9, bytes_accessed=2**23, transcendentals=10**7)

    def attend(away, visitor, extra):
        kernel = functools.partial(attend_kernel, away, n, bool(extra))
        return call(kernel, (meta, visitor, k, v, live) + extra, shape, scratch, cost)

    back = [shift(attend(d, visitors[d - 1], ()), 2 * d, n) for d in (1, 2)]
    parts = (attend(0, q, tail), *back)
    done = call(finish_kernel, (meta,) + parts, jax.ShapeDtypeStruct(q.shape, bf))
    mine = lax.dynamic_slice_in_dim(done, core * BLOCK, BLOCK, axis=0)
    other = flip(lax.dynamic_slice_in_dim(done, (1 - core) * BLOCK, BLOCK, axis=0), n)
    return jnp.where(
        core == 0,
        jnp.concatenate([mine, other], axis=1),
        jnp.concatenate([other, mine], axis=1),
    )


def solution(mesh):
    placed = (
        P(("groups", "seq"), None),
        P(("groups", "seq"), None),
        P(("groups", "seq"), None),
        P(("groups", "seq")),
        P(("groups", "seq"), None),
    )
    return jax.shard_map(
        body, mesh=mesh, in_specs=placed, out_specs=P(("groups", "seq"), None), check_vma=False
    )
```

time: 493 us -> 142 us (0.29)
  the two profiles are of different devices: /device:TPU:28 before, /device:TPU:21 now
where the time goes in v1:
time: 142 us
  Pallas kernels  50.4 us (35%)
  waiting for transfers between devices  35.2 us (25%)
  starting transfers between devices  23.1 us (16%)
  blocking collectives  15.7 us (11%)
  local copies, waits for them, and re-layouts  13.5 us (10%)
  other arithmetic  2.9 us (2%)
    pallas_call x6, Pallas kernels, call(): pl.pallas_call(kernel, out_shape=shapes, in_specs=[SMEM] + [VMEM] * (len(...  50.4 us
    ppermute x5, waiting for transfers between devices, shift(): return lax.ppermute(array, 'seq', pairs)  33.7 us
    ppermute x5, starting transfers between devices, shift(): return lax.ppermute(array, 'seq', pairs)  20.2 us
    all_gather x1, blocking collectives, body(): meta = lax.all_gather(own, 'seq', axis=0, tiled=True).reshape(-1)  15.7 us
    dynamic_slice x3, local copies, waits for them, and re-layouts, half_of(): return lax.dynamic_slice_in_dim(array, which * width, width, axis=1)  6.1 us
    ppermute x4, starting transfers between devices, flip(): return lax.ppermute(array, 'seq', [(i, i ^ 1) for i in range(n)])  2.92 us
  transfers between devices with their start and end apart: 9, of which 4 were waited for; matrix products, arithmetic and copies ran while one was open for 7% of the time, Pallas kernels for 35%

profile of v1, /device:TPU:21, one launch (start us, length us, event | category | flops | bytes accessed | tf_op | source)
XLA Modules:
  0.0 141.7 jit_solution(8328083251359865061)
XLA Ops:
  0.0 2.1 %constant_dynamic-slice_fusion.6 = (bf16[256,1024]{1,0:T(8,128)(2,1)}, bf16[256,1024]{1,0:T(8,128)(2,1)S(1)}) fusion(bf16[256,2048]{1,0:T(8,128)(2,1)} %param.5, s32[]{:T(128)S(6)} %select_n.38, s32[]{:T(128)S(6)} %select_n.37), kind=kLoop, calls=%fused_computation.8 | loop fusion | bytes 2097160 | tf_op jit(solution)/shard_map/dynamic_slice | solution.py:274
  2.7 2.8 %constant_dynamic-slice_fusion.4 = (bf16[1024,512]{1,0:T(8,128)(2,1)}, bf16[1024,512]{1,0:T(8,128)(2,1)S(1)}) fusion(bf16[1024,1024]{1,0:T(8,128)(2,1)} %param.6, s32[]{:T(128)S(6)} %select_n.40, s32[]{:T(128)S(6)} %select_n.39), kind=kLoop, calls=%fused_computation.6 | loop fusion | bytes 4194312 | tf_op jit(solution)/shard_map/dynamic_slice | solution.py:274
  5.6 1.2 constant_dynamic-slice_fusion.2
  8.0 15.7 %all-gather = s32[16,1,3]{2,1,0:T(1,128)S(1)} all-gather(s32[1,1,3]{2,1,0:T(1,128)S(1)} %add_bitcast_fusion), channel_id=1, replica_groups=mesh['groups'=2,'seq'=16] {'seq'}, dimensions={0}, use_global_device_ids=true | all-gather | bytes 204 | tf_op jit(solution)/shard_map/all_gather | solution.py:282
  24.9 2.4 %shard_map.55.q_ref = bf16[512,1024]{1,0:T(8,128)(2,1)S(1)} custom-call(s32[48]{0:T(128)S(1)} %reshape.3.meta, bf16[256,1024]{1,0:T(8,128)(2,1)S(1)} %get-tuple-element.18.mine, bf16[256,1024]{1,0:T(8,128)(2,1)S(1)} %collective-permute-done.other), custom_call_target="tpu_custom_call" | custom-call | flops 10000000 | bytes 2097152 | tf_op jit(solution)/shard_map/pallas_call | solution.py:252
  27.3 4.8 %collective-permute-start.6 = (bf16[512,1024]{1,0:T(8,128)(2,1)S(1)}, bf16[512,1024]{1,0:T(8,128)(2,1)S(1)}, u32[]{:S(2)}, u32[]{:S(2)}) collective-permute-start(bf16[512,1024]{1,0:T(8,128)(2,1)S(1)} %shard_map.55.q_ref), channel_id=1, source_target_pairs={{4,0},{5,1},{6,2},{7,3},{8,4},{9,5},{10,6},{11,7},{12,8},{13,9},{1... | collective-permute-start | bytes 3145736 | tf_op jit(solution)/shard_map/ppermute | solution.py:265
  32.2 2.1 %collective-permute-start.4 = (bf16[512,1024]{1,0:T(8,128)(2,1)S(1)}, bf16[512,1024]{1,0:T(8,128)(2,1)S(1)}, u32[]{:S(2)}, u32[]{:S(2)}) collective-permute-start(bf16[512,1024]{1,0:T(8,128)(2,1)S(1)} %shard_map.55.q_ref), channel_id=1, source_target_pairs={{2,0},{3,1},{4,2},{5,3},{6,4},{7,5},{8,6},{9,7},{10,8},{11,9},{12,... | collective-permute-start | bytes 3145736 | tf_op jit(solution)/shard_map/ppermute | solution.py:265
  34.3 9.7 %shard_map.56 = (bf16[2048,512]{1,0:T(8,128)(2,1)}, bf16[2048,512]{1,0:T(8,128)(2,1)}, bf16[2048,128]{1,0:T(8,128)(2,1)S(1)}) custom-call(s32[48]{0:T(128)S(1)} %reshape.3.meta, bf16[1024,512]{1,0:T(8,128)(2,1)S(1)} %get-tuple-element.14.k_mine, bf16[1024,512]{1,0:T(8,128)(2,1)} %collective-permute-done.1.k_other, ...), custom_call_target="tpu_custom_call" | custom-call | flops 100000000 | bytes 8388608 | tf_op jit(solution)/shard_map/pallas_call | solution.py:252
  44.0 1.2 slice.18
  47.1 1.9 %collective-permute-start.3 = (bf16[256,1152]{1,0:T(8,128)(2,1)}, bf16[256,1152]{1,0:T(8,128)(2,1)}, u32[]{:S(2)}, u32[]{:S(2)}) collective-permute-start(bf16[256,1152]{1,0:T(8,128)(2,1)} %pad_maximum_fusion), channel_id=1, source_target_pairs={{0,6},{1,7},{2,8},{3,9},{4,10},{5,11},{6,12},{7,13},{8,14},{9,15},... | collective-permute-start | bytes 1769480 | tf_op jit(solution)/shard_map/ppermute | solution.py:265
  49.0 5.5 %collective-permute-done.6.q_ref = bf16[512,1024]{1,0:T(8,128)(2,1)S(1)} collective-permute-done((bf16[512,1024]{1,0:T(8,128)(2,1)S(1)}, bf16[512,1024]{1,0:T(8,128)(2,1)S(1)}, u32[]{:S(2)}, u32[]{:S(2)}) %collective-permute-start.6) | collective-permute-done | bytes 1048608 | tf_op jit(solution)/shard_map/ppermute | solution.py:265
  54.5 15.4 %shard_map.59 = bf16[512,1152]{1,0:T(8,128)(2,1)} custom-call(s32[48]{0:T(128)S(1)} %reshape.3.meta, bf16[512,1024]{1,0:T(8,128)(2,1)S(1)} %collective-permute-done.6.q_ref, bf16[2048,512]{1,0:T(8,128)(2,1)S(1)} %copy-done.2, bf16[2048,512]{1,0:T(8,128)(2,1)} %get-tuple-element.9.v_ref, bf16[2048,128]{1,0:T(8,128)(2,1)S(1)} %get-tuple-element.10.live_ref), custom_call_target="tpu_custom_call" | custom-call | flops 6000000000 | bytes 8388608 | tf_op jit(solution)/shard_map/pallas_call | solution.py:252
  69.9 2.0 %collective-permute-start.7 = (bf16[512,1152]{1,0:T(8,128)(2,1)}, bf16[512,1152]{1,0:T(8,128)(2,1)S(1)}, u32[]{:S(2)}, u32[]{:S(2)}) collective-permute-start(bf16[512,1152]{1,0:T(8,128)(2,1)} %shard_map.59), channel_id=1, source_target_pairs={{0,4},{1,5},{2,6},{3,7},{4,8},{5,9},{6,10},{7,11},{8,12},{9,13},{1... | collective-permute-start | bytes 3538952 | tf_op jit(solution)/shard_map/ppermute | solution.py:265
  71.9 16.0 %collective-permute-done.4.q_ref = bf16[512,1024]{1,0:T(8,128)(2,1)S(1)} collective-permute-done((bf16[512,1024]{1,0:T(8,128)(2,1)S(1)}, bf16[512,1024]{1,0:T(8,128)(2,1)S(1)}, u32[]{:S(2)}, u32[]{:S(2)}) %collective-permute-start.4) | collective-permute-done | bytes 1048608 | tf_op jit(solution)/shard_map/ppermute | solution.py:265
  88.0 10.2 %shard_map.58 = bf16[512,1152]{1,0:T(8,128)(2,1)} custom-call(s32[48]{0:T(128)S(1)} %reshape.3.meta, bf16[512,1024]{1,0:T(8,128)(2,1)S(1)} %collective-permute-done.4.q_ref, bf16[2048,512]{1,0:T(8,128)(2,1)S(1)} %copy-done.2, bf16[2048,512]{1,0:T(8,128)(2,1)} %get-tuple-element.9.v_ref, bf16[2048,128]{1,0:T(8,128)(2,1)S(1)} %get-tuple-element.10.live_ref), custom_call_target="tpu_custom_call" | custom-call | flops 6000000000 | bytes 8388608 | tf_op jit(solution)/shard_map/pallas_call | solution.py:252
  98.2 9.3 %collective-permute-start.5 = (bf16[512,1152]{1,0:T(8,128)(2,1)}, bf16[512,1152]{1,0:T(8,128)(2,1)S(1)}, u32[]{:S(2)}, u32[]{:S(2)}) collective-permute-start(bf16[512,1152]{1,0:T(8,128)(2,1)} %shard_map.58), channel_id=1, source_target_pairs={{0,2},{1,3},{2,4},{3,5},{4,6},{5,7},{6,8},{7,9},{8,10},{9,11},{10,... | collective-permute-start | bytes 3538952 | tf_op jit(solution)/shard_map/ppermute | solution.py:265
  108.3 1.1 fusion
  109.4 1.6 %copy-done.3 = bf16[2048,512]{1,0:T(8,128)(2,1)S(1)} copy-done((bf16[2048,512]{1,0:T(8,128)(2,1)S(1)}, bf16[2048,512]{1,0:T(8,128)(2,1)}, u32[]{:S(2)}) %copy-start.3) | copy-done | bytes 2097176
  112.0 11.3 %shard_map.57.refs_0_ = bf16[512,1152]{1,0:T(8,128)(2,1)S(1)} custom-call(s32[48]{0:T(128)S(1)} %reshape.3.meta, bf16[512,1024]{1,0:T(8,128)(2,1)S(1)} %copy-done.1, bf16[2048,512]{1,0:T(8,128)(2,1)S(1)} %copy-done.3, bf16[2048,512]{1,0:T(8,128)(2,1)} %get-tuple-element.9.v_ref, bf16[2048,128]{1,0:T(8,128)(2,1)S(1)} %copy-done.5, ...), custom_call_target="tpu_custom_call" | custom-call | flops 6000000000 | bytes 8388608 | tf_op jit(solution)/shard_map/pallas_call | solution.py:252
  123.3 12.1 %collective-permute-done.5.refs_1_ = bf16[512,1152]{1,0:T(8,128)(2,1)S(1)} collective-permute-done((bf16[512,1152]{1,0:T(8,128)(2,1)}, bf16[512,1152]{1,0:T(8,128)(2,1)S(1)}, u32[]{:S(2)}, u32[]{:S(2)}) %collective-permute-start.5) | collective-permute-done | bytes 1179680 | tf_op jit(solution)/shard_map/ppermute | solution.py:265
  135.4 1.5 %shard_map.60 = bf16[512,1024]{1,0:T(8,128)(2,1)S(1)} custom-call(s32[48]{0:T(128)S(1)} %reshape.3.meta, bf16[512,1152]{1,0:T(8,128)(2,1)S(1)} %shard_map.57.refs_0_, bf16[512,1152]{1,0:T(8,128)(2,1)S(1)} %collective-permute-done.5.refs_1_, bf16[512,1152]{1,0:T(8,128)(2,1)S(1)} %collective-permute-done.7.refs_2_), custom_call_target="tpu_custom_call" | custom-call | tf_op jit(solution)/shard_map/pallas_call | solution.py:252
  137.0 1.7 %collective-permute-start.8 = (bf16[256,1024]{1,0:T(8,128)(2,1)S(1)}, bf16[256,1024]{1,0:T(8,128)(2,1)S(1)}, u32[]{:S(2)}, u32[]{:S(2)}) collective-permute-start(bf16[256,1024]{1,0:T(8,128)(2,1)S(1)} %get-tuple-element.16), channel_id=1, source_target_pairs={{0,1},{1,0},{2,3},{3,2},{4,5},{5,4},{6,7},{7,6},{8,9},{9,8},{10,11... | collective-permute-start | bytes 1572872 | tf_op jit(solution)/shard_map/ppermute | solution.py:269
  138.8 1.5 %collective-permute-done.8 = bf16[256,1024]{1,0:T(8,128)(2,1)S(1)} collective-permute-done((bf16[256,1024]{1,0:T(8,128)(2,1)S(1)}, bf16[256,1024]{1,0:T(8,128)(2,1)S(1)}, u32[]{:S(2)}, u32[]{:S(2)}) %collective-permute-start.8) | collective-permute-done | bytes 524320 | tf_op jit(solution)/shard_map/ppermute | solution.py:269
  140.3 1.4 maximum_select_fusion
  (32 shorter events, 6.3 us)
Async XLA Ops:
  2.1 22.8 %collective-permute-start = (bf16[256,1024]{1,0:T(8,128)(2,1)}, bf16[256,1024]{1,0:T(8,128)(2,1)S(1)}, u32[]{:S(2)}, u32[]{:S(2)}) collective-permute-start(bf16[256,1024]{1,0:T(8,128)(2,1)} %get-tuple-element.17), channel_id=1, source_target_pairs={{0,1},{1,0},{2,3},{3,2},{4,5},{5,4},{6,7},{7,6},{8,9},{9,8},{10,11... | collective-permute-start | bytes 1572872 | tf_op jit(solution)/shard_map/ppermute | solution.py:269
  2.7 2.8 %copy-start.6 = (bf16[1024,1024]{1,0:T(8,128)(2,1)S(1)}, bf16[1024,1024]{1,0:T(8,128)(2,1)}, u32[]{:S(2)}) copy-start(bf16[1024,1024]{1,0:T(8,128)(2,1)} %param.7) | copy-start | bytes 6291460
  5.6 2.4 %copy-start.7 = (s32[1,2]{1,0:T(1,128)S(1)}, s32[1,2]{1,0:T(1,128)}, u32[]{:S(2)}) copy-start(s32[1,2]{1,0:T(1,128)} %param.9) | copy-start | bytes 28
  5.6 28.7 %collective-permute-start.1 = (bf16[1024,512]{1,0:T(8,128)(2,1)}, bf16[1024,512]{1,0:T(8,128)(2,1)}, u32[]{:S(2)}, u32[]{:S(2)}) collective-permute-start(bf16[1024,512]{1,0:T(8,128)(2,1)} %get-tuple-element.13), channel_id=1, source_target_pairs={{0,1},{1,0},{2,3},{3,2},{4,5},{5,4},{6,7},{7,6},{8,9},{9,8},{10,11... | collective-permute-start | bytes 3145736 | tf_op jit(solution)/shard_map/ppermute | solution.py:269
  6.8 27.5 %collective-permute-start.2 = (bf16[1024,512]{1,0:T(8,128)(2,1)}, bf16[1024,512]{1,0:T(8,128)(2,1)}, u32[]{:S(2)}, u32[]{:S(2)}) collective-permute-start(bf16[1024,512]{1,0:T(8,128)(2,1)} %get-tuple-element.11), channel_id=1, source_target_pairs={{0,1},{1,0},{2,3},{3,2},{4,5},{5,4},{6,7},{7,6},{8,9},{9,8},{10,11... | collective-permute-start | bytes 3145736 | tf_op jit(solution)/shard_map/ppermute | solution.py:269
  27.3 16.7 %copy-start = (bf16[512,1024]{1,0:T(8,128)(2,1)}, bf16[512,1024]{1,0:T(8,128)(2,1)S(1)}, u32[]{:S(2)}) copy-start(bf16[512,1024]{1,0:T(8,128)(2,1)S(1)} %shard_map.55.q_ref) | copy-start | bytes 3145732
  27.3 27.2 %collective-permute-start.6 = (bf16[512,1024]{1,0:T(8,128)(2,1)S(1)}, bf16[512,1024]{1,0:T(8,128)(2,1)S(1)}, u32[]{:S(2)}, u32[]{:S(2)}) collective-permute-start(bf16[512,1024]{1,0:T(8,128)(2,1)S(1)} %shard_map.55.q_ref), channel_id=1, source_target_pairs={{4,0},{5,1},{6,2},{7,3},{8,4},{9,5},{10,6},{11,7},{12,8},{13,9},{1... | collective-permute-start | bytes 3145736 | tf_op jit(solution)/shard_map/ppermute | solution.py:265
  32.2 55.8 %collective-permute-start.4 = (bf16[512,1024]{1,0:T(8,128)(2,1)S(1)}, bf16[512,1024]{1,0:T(8,128)(2,1)S(1)}, u32[]{:S(2)}, u32[]{:S(2)}) collective-permute-start(bf16[512,1024]{1,0:T(8,128)(2,1)S(1)} %shard_map.55.q_ref), channel_id=1, source_target_pairs={{2,0},{3,1},{4,2},{5,3},{6,4},{7,5},{8,6},{9,7},{10,8},{11,9},{12,... | collective-permute-start | bytes 3145736 | tf_op jit(solution)/shard_map/ppermute | solution.py:265
  44.0 44.0 %copy-start.4 = (bf16[2048,128]{1,0:T(8,128)(2,1)}, bf16[2048,128]{1,0:T(8,128)(2,1)S(1)}, u32[]{:S(2)}) copy-start(bf16[2048,128]{1,0:T(8,128)(2,1)S(1)} %get-tuple-element.10.live_ref) | copy-start | bytes 1572868
  44.0 10.5 %copy-start.2 = (bf16[2048,512]{1,0:T(8,128)(2,1)S(1)}, bf16[2048,512]{1,0:T(8,128)(2,1)}, u32[]{:S(2)}) copy-start(bf16[2048,512]{1,0:T(8,128)(2,1)} %get-tuple-element.8.k_ref) | copy-start | bytes 6291460
  47.1 60.4 %collective-permute-start.3 = (bf16[256,1152]{1,0:T(8,128)(2,1)}, bf16[256,1152]{1,0:T(8,128)(2,1)}, u32[]{:S(2)}, u32[]{:S(2)}) collective-permute-start(bf16[256,1152]{1,0:T(8,128)(2,1)} %pad_maximum_fusion), channel_id=1, source_target_pairs={{0,6},{1,7},{2,8},{3,9},{4,10},{5,11},{6,12},{7,13},{8,14},{9,15},... | collective-permute-start | bytes 1769480 | tf_op jit(solution)/shard_map/ppermute | solution.py:265
  69.9 39.5 %copy-start.1 = (bf16[512,1024]{1,0:T(8,128)(2,1)S(1)}, bf16[512,1024]{1,0:T(8,128)(2,1)}, u32[]{:S(2)}) copy-start(bf16[512,1024]{1,0:T(8,128)(2,1)} %copy-done) | copy-start | bytes 3145732
  69.9 53.4 %collective-permute-start.7 = (bf16[512,1152]{1,0:T(8,128)(2,1)}, bf16[512,1152]{1,0:T(8,128)(2,1)S(1)}, u32[]{:S(2)}, u32[]{:S(2)}) collective-permute-start(bf16[512,1152]{1,0:T(8,128)(2,1)} %shard_map.59), channel_id=1, source_target_pairs={{0,4},{1,5},{2,6},{3,7},{4,8},{5,9},{6,10},{7,11},{8,12},{9,13},{1... | collective-permute-start | bytes 3538952 | tf_op jit(solution)/shard_map/ppermute | solution.py:265
  98.2 37.2 %collective-permute-start.5 = (bf16[512,1152]{1,0:T(8,128)(2,1)}, bf16[512,1152]{1,0:T(8,128)(2,1)S(1)}, u32[]{:S(2)}, u32[]{:S(2)}) collective-permute-start(bf16[512,1152]{1,0:T(8,128)(2,1)} %shard_map.58), channel_id=1, source_target_pairs={{0,2},{1,3},{2,4},{3,5},{4,6},{5,7},{6,8},{7,9},{8,10},{9,11},{10,... | collective-permute-start | bytes 3538952 | tf_op jit(solution)/shard_map/ppermute | solution.py:265
  109.4 1.6 %copy-start.3 = (bf16[2048,512]{1,0:T(8,128)(2,1)S(1)}, bf16[2048,512]{1,0:T(8,128)(2,1)}, u32[]{:S(2)}) copy-start(bf16[2048,512]{1,0:T(8,128)(2,1)} %get-tuple-element.8.k_ref) | copy-start | bytes 6291460
  111.0 1.0 copy-start.5
  137.0 3.3 %collective-permute-start.8 = (bf16[256,1024]{1,0:T(8,128)(2,1)S(1)}, bf16[256,1024]{1,0:T(8,128)(2,1)S(1)}, u32[]{:S(2)}, u32[]{:S(2)}) collective-permute-start(bf16[256,1024]{1,0:T(8,128)(2,1)S(1)} %get-tuple-element.16), channel_id=1, source_target_pairs={{0,1},{1,0},{2,3},{3,2},{4,5},{5,4},{6,7},{7,6},{8,9},{9,8},{10,11... | collective-permute-start | bytes 1572872 | tf_op jit(solution)/shard_map/ppermute | solution.py:269

commit v2 on v0

v2 whole, which is shorter than its diff:
```python
import functools
import math

import jax
import jax.numpy as jnp
from jax import lax
from jax.experimental import pallas as pl
from jax.experimental.pallas import tpu as pltpu
from jax.sharding import PartitionSpec as P

HEAD = 128
WINDOW = 4096
BLOCK = 256
CAP = 50.0
QUERY_SCALE = 144.0 ** (-0.5)
LOG2E = math.log2(math.e)
VMEM = pl.BlockSpec(memory_space=pltpu.VMEM)
ANY = pl.BlockSpec(memory_space=pl.ANY)
SMEM = pl.BlockSpec(memory_space=pltpu.SMEM)
MESH = pl.DeviceIdType.MESH


def removed_before(meta, shard):
    def add(s, total):
        return total + meta[3 * s + 2] - meta[3 * s + 1]

    return lax.fori_loop(0, shard, add, jnp.int32(0))


def tables(row, base, begin, length):
    lane = lax.broadcasted_iota(jnp.int32, row.shape, 1)
    order = (lane % (HEAD // 2)).astype(jnp.float32)
    freq = jnp.exp(order * (-2.0 * math.log(10000.0) / HEAD))
    place = row - base - jnp.clip(row - begin, 0, length)
    angle = place.astype(jnp.float32) * freq
    low = lane < HEAD // 2
    cosine, sine = jnp.cos(angle), jnp.sin(angle)
    cosine_swap = pltpu.roll(cosine, HEAD // 2, 1)
    sine_swap = pltpu.roll(sine, HEAD // 2, 1)
    return (
        (jnp.where(low, cosine, cosine_swap), jnp.where(low, -sine, sine_swap)),
        (jnp.where(low, cosine_swap, cosine), jnp.where(low, -sine_swap, sine)),
    )


def rotate(x, table):
    x = x.astype(jnp.float32)
    return x * table[0] + pltpu.roll(x, HEAD // 2, 1) * table[1]


def at_seq(device):
    return {"seq": device}


def greet(conditions_devices):
    barrier = pltpu.get_barrier_semaphore()
    count = jnp.int32(0)
    for condition, device in conditions_devices:

        @pl.when(condition)
        def _():
            pl.semaphore_signal(barrier, inc=1, device_id=at_seq(device), device_id_type=MESH)

        count = count + jnp.where(condition, 1, 0)
    pl.semaphore_wait(barrier, count)


def exchange_kernel(n, own, q, k, v, meta, q_all, k_all, v_all, meta_sems, sems, local_sems):
    me = lax.axis_index("seq")
    core = lax.rem(me, 2)
    peer = me + 1 - 2 * core
    barrier = pltpu.get_barrier_semaphore()

    @pl.loop(1, n)
    def _(i):
        target = lax.rem(me + i, n)
        pl.semaphore_signal(barrier, inc=1, device_id=at_seq(target), device_id_type=MESH)

    pl.semaphore_wait(barrier, n - 1)

    def meta_copy(i, owner, target):
        return pltpu.make_async_remote_copy(
            src_ref=own,
            dst_ref=meta.at[owner],
            send_sem=meta_sems.at[0, i],
            recv_sem=meta_sems.at[1, owner],
            device_id=at_seq(target),
            device_id_type=MESH,
        )

    @pl.loop(1, n)
    def _(i):
        meta_copy(i, me, lax.rem(me + i, n)).start()

    copies = []
    for index, (source, target) in enumerate(((q, q_all), (k, k_all), (v, v_all))):
        rows, width = source.shape[0], source.shape[1] // 2
        theirs = pl.ds(pl.multiple_of((1 - core) * width, HEAD), width)
        mine = pl.ds(pl.multiple_of(core * width, HEAD), width)
        to = pl.ds(pl.multiple_of(core * rows, BLOCK), rows)
        remote = pltpu.make_async_remote_copy(
            src_ref=source.at[:, theirs],
            dst_ref=target.at[to, :],
            send_sem=sems.at[0, index],
            recv_sem=sems.at[1, index],
            device_id=at_seq(peer),
            device_id_type=MESH,
        )
        remote.start()
        local = pltpu.make_async_copy(source.at[:, mine], target.at[to, :], local_sems.at[index])
        local.start()
        copies += [remote, local]
    local = pltpu.make_async_copy(own, meta.at[me], local_sems.at[3])
    local.start()
    for copy in copies + [local]:
        copy.wait()

    @pl.loop(1, n)
    def _(i):
        meta_copy(i, me, lax.rem(me + i, n)).wait_send()
        sender = lax.rem(me + n - i, n)
        meta_copy(i, sender, sender).wait_recv()


def rope_q(meta, shard, slot, raw_rows, source, out):
    half = BLOCK // 2
    block = jnp.maximum(meta[3 * shard], 0)
    begin = meta[3 * shard + 1]
    length = meta[3 * shard + 2] - begin
    base = removed_before(meta, shard)
    raw0 = shard * raw_rows + block * BLOCK
    tile = 32

    @pl.loop(0, half // tile)
    def _(step):
        at = step * tile
        row = lax.broadcasted_iota(jnp.int32, (tile, HEAD), 0) + raw0 + at
        lane = lax.broadcasted_iota(jnp.int32, (tile, HEAD), 1)
        row = row + jnp.where(lane < HEAD // 2, 0, half)
        both = tables(row, base, begin, length)
        for part in range(2):
            rows = pl.ds(pl.multiple_of(slot * BLOCK + at + part * half, tile), tile)
            here = pl.ds(pl.multiple_of(at + part * half, tile), tile)
            for h in range(out.shape[1] // HEAD):
                cols = pl.ds(h * HEAD, HEAD)
                x = rotate(source[rows, cols], both[part]) * QUERY_SCALE
                out[here, cols] = x.astype(jnp.bfloat16)


def prepare(meta, shard, slot, k_ref, v_ref, k_out, v_out, live_out):
    rows = k_ref.shape[0] // 2
    half = rows // 2
    begin = meta[3 * shard + 1]
    finish = meta[3 * shard + 2]
    base = removed_before(meta, shard)
    raw0 = shard * rows
    tile = 32

    @pl.loop(0, half // tile)
    def _(step):
        at = step * tile
        iota = lax.broadcasted_iota(jnp.int32, (tile, HEAD), 0)
        lane = lax.broadcasted_iota(jnp.int32, (tile, HEAD), 1)
        row = iota + raw0 + at + jnp.where(lane < HEAD // 2, 0, half)
        both = tables(row, base, begin, finish - begin)
        for part in range(2):
            src = at + part * half
            place = pl.ds(pl.multiple_of(slot * rows + src, tile), tile)
            raw = iota + raw0 + src
            live = jnp.where((raw >= begin) & (raw < finish), 0.0, 1.0)
            live_out[place, :] = live.astype(jnp.bfloat16)
            for h in range(k_out.shape[1] // HEAD):
                cols = pl.ds(h * HEAD, HEAD)
                x = rotate(k_ref[place, cols], both[part])
                k_out[place, cols] = x.astype(jnp.bfloat16)
                y = v_ref[place, cols].astype(jnp.float32) * live
                v_out[place, cols] = y.astype(jnp.bfloat16)


def visit(q_ref, k_ref, v_ref, live_ref, acc, at, size, mask):
    kv_heads = k_ref.shape[1] // HEAD
    rows = pl.ds(at if isinstance(at, int) else pl.multiple_of(at, BLOCK), size)

    def scores(h):
        q = jnp.concatenate(
            [q_ref[:, pl.ds((2 * h + g) * HEAD, HEAD)] for g in range(2)], axis=0
        )
        k = k_ref[rows, pl.ds(h * HEAD, HEAD)]
        return lax.dot_general(
            q, k, (((1,), (1,)), ((), ())), preferred_element_type=jnp.float32
        )

    s = scores(0)
    for h in range(kv_heads):
        ahead = scores(h + 1) if h + 1 < kv_heads else None
        weight = jnp.exp2(jnp.tanh(s * (1.0 / CAP)) * (CAP * LOG2E))
        if mask is not None:
            weight = jnp.where(mask, weight, 0.0)
        v = jnp.concatenate([v_ref[rows, pl.ds(h * HEAD, HEAD)], live_ref[rows, :]], axis=1)
        acc[h] += jnp.dot(weight.astype(jnp.bfloat16), v, preferred_element_type=jnp.float32)
        s = ahead


def allowed(meta, n, shard_q, shard_k, raw_rows, at_k, size):
    shard_q = jnp.clip(shard_q, 0, n - 1)
    shard_k = jnp.clip(shard_k, 0, n - 1)
    column = lax.broadcasted_iota(jnp.int32, (2 * BLOCK, 1), 0)
    raw_q = shard_q * raw_rows + jnp.maximum(meta[3 * shard_q], 0) * BLOCK
    q = raw_q + jnp.where(column < BLOCK, column, column - BLOCK)
    k = shard_k * raw_rows + at_k + lax.broadcasted_iota(jnp.int32, (1, size), 1)
    begin_q, end_q = meta[3 * shard_q + 1], meta[3 * shard_q + 2]
    begin_k, end_k = meta[3 * shard_k + 1], meta[3 * shard_k + 2]
    between = removed_before(meta, shard_q) - removed_before(meta, shard_k)
    q_place = q - between - jnp.clip(q - begin_q, 0, end_q - begin_q)
    k_place = k - jnp.clip(k - begin_k, 0, end_k - begin_k)
    return (k <= q) & (q_place - k_place < WINDOW)


def pack(acc, out):
    kv_heads = acc.shape[0]
    lane = lax.broadcasted_iota(jnp.int32, (BLOCK, HEAD), 1)
    packed = jnp.zeros((BLOCK, HEAD), jnp.float32)
    for h in range(kv_heads):
        for part in range(2):
            head = 2 * h + part
            mine = pl.ds(part * BLOCK, BLOCK)
            out[:, pl.ds(head * HEAD, HEAD)] = acc[h, mine, pl.ds(0, HEAD)].astype(jnp.bfloat16)
            total = acc[h, mine, pl.ds(HEAD, HEAD)]
            coarse = total.astype(jnp.bfloat16).astype(jnp.float32)
            packed = jnp.where(lane == head, coarse, packed)
            packed = jnp.where(lane == head + 2 * kv_heads, total - coarse, packed)
    out[:, pl.ds(2 * kv_heads * HEAD, HEAD)] = packed.astype(jnp.bfloat16)


def finish(meta, shard, raw_rows, parts, out):
    heads = out.shape[1] // HEAD
    block = meta[3 * shard]
    begin, end = meta[3 * shard + 1], meta[3 * shard + 2]
    raw0 = shard * raw_rows + jnp.maximum(block, 0) * BLOCK
    tile = 64

    @pl.loop(0, BLOCK // tile)
    def _(step):
        here = pl.ds(pl.multiple_of(step * tile, tile), tile)
        raw = raw0 + step * tile + lax.broadcasted_iota(jnp.int32, (tile, HEAD), 0)
        keep = ((raw < begin) | (raw >= end)) & (block >= 0)
        totals = jnp.zeros((tile, HEAD), jnp.float32)
        for part in parts:
            totals += part[here, pl.ds(heads * HEAD, HEAD)].astype(jnp.float32)
        for h in range(heads):
            cols = pl.ds(h * HEAD, HEAD)
            total = totals[:, h : h + 1] + totals[:, heads + h : heads + h + 1]
            total = jnp.broadcast_to(jnp.where(total > 0, total, 1.0), (tile, HEAD))
            value = jnp.zeros((tile, HEAD), jnp.float32)
            for part in parts:
                value += part[here, cols].astype(jnp.float32)
            out[here, cols] = jnp.where(keep, value / total, 0.0).astype(jnp.bfloat16)


def serve_kernel(
    n, reach, meta, q_raw, k_raw, v_raw, out,
    q, k, v, live, q_in, part_out, part_in, own, tail_k, tail_v, tail_live, acc, done, give_away, got,
    q_sems, part_sems, tail_sems, done_sems,
):
    me = lax.axis_index("seq")
    core = lax.rem(me, 2)
    chip = lax.div(me, 2)
    chips = n // 2
    peer = me + 1 - 2 * core
    rows = k.shape[0] // 2
    per = rows // BLOCK
    far = reach + 1
    wide = 2 * BLOCK
    first = 2 * chip
    greet(
        [(me >= 0, peer)]
        + [(chip >= d, me - 2 * d) for d in range(1, far + 1)]
        + [(chip + d < chips, me + 2 * d) for d in range(1, far + 1)]
    )

    def q_copy(d, slot):
        return pltpu.make_async_remote_copy(
            src_ref=q[slot],
            dst_ref=q_in[2 * d - 2 + slot],
            send_sem=q_sems.at[0, d - 1, slot],
            recv_sem=q_sems.at[1, d - 1, slot],
            device_id=at_seq(jnp.maximum(me - 2 * d, core)),
            device_id_type=MESH,
        )

    def part_copy(d, slot):
        return pltpu.make_async_remote_copy(
            src_ref=part_out[2 * d - 2 + slot],
            dst_ref=part_in[2 * d - 2 + slot],
            send_sem=part_sems.at[0, d - 1, slot],
            recv_sem=part_sems.at[1, d - 1, slot],
            device_id=at_seq(jnp.minimum(me + 2 * d, n - 2 + core)),
            device_id_type=MESH,
        )

    last = pl.ds(2 * rows - BLOCK, BLOCK)
    tails = [
        pltpu.make_async_remote_copy(
            src_ref=source.at[last, :],
            dst_ref=target,
            send_sem=tail_sems.at[0, i],
            recv_sem=tail_sems.at[1, i],
            device_id=at_seq(jnp.minimum(me + 2 * far, n - 2 + core)),
            device_id_type=MESH,
        )
        for i, (source, target) in enumerate(((k, tail_k), (v, tail_v), (live, tail_live)))
    ]

    for slot in range(2):
        rope_q(meta, first + slot, slot, rows, q_raw, q[slot])
    for slot in range(2):
        for d in range(1, reach + 1):

            @pl.when(chip >= d)
            def _():
                q_copy(d, slot).start()

    for d in range(1, reach + 1):

        @pl.when(chip < d)
        def _():
            for ref in part_in[2 * d - 2 : 2 * d]:
                ref[...] = jnp.zeros_like(ref)

    @pl.loop(0, 2)
    def _(i):
        slot = 1 - i
        prepare(meta, first + slot, slot, k_raw, v_raw, k, v, live)

    @pl.when(chip + far < chips)
    def _():
        for copy in tails:
            copy.start()

    def masked(source, shard_q, j, size):
        shard_k = first + lax.div(j, per)
        mask = allowed(meta, n, shard_q, shard_k, rows, lax.rem(j, per) * BLOCK, size)
        visit(source, k, v, live, acc, j * BLOCK, size, mask)

    def plain(source, j):
        visit(source, k, v, live, acc, j * BLOCK, wide, None)

    def own_part(slot):
        acc[...] = jnp.zeros_like(acc)
        if slot == 1:

            @pl.loop(0, per // 2)
            def _(i):
                plain(q[slot], 2 * i)

        @pl.loop(0, per // 2)
        def _(i):
            masked(q[slot], first + slot, slot * per + 2 * i, wide)

    own_part(1)
    pack(acc, own[1])

    for d in range(1, reach + 1):

        @pl.when(chip + d < chips)
        def _():
            for slot in range(2):
                source = q_in[2 * d - 2 + slot]
                q_copy(d, slot).wait_recv()
                acc[...] = jnp.zeros_like(acc)
                if d < reach:

                    @pl.loop(0, per)
                    def _(i):
                        plain(source, 2 * i)

                else:
                    shard_q = first + 2 * d + slot

                    @pl.loop(0, per // 2)
                    def _(i):
                        masked(source, shard_q, slot * per + 2 * i, wide)

                    if slot == 0:

                        @pl.loop(0, per // 2)
                        def _(i):
                            plain(source, per + 2 * i)

                    else:
                        masked(source, shard_q, jnp.int32(per - 1), BLOCK)

                pack(acc, part_out[2 * d - 2 + slot])
                part_copy(d, slot).start()

    own_part(0)

    @pl.when(chip >= far)
    def _():
        for copy in tails:
            copy.wait_recv()
        mask = allowed(meta, n, first, first - 2 * far + 1, rows, rows - BLOCK, BLOCK)
        visit(q[0], tail_k, tail_v, tail_live, acc, 0, BLOCK, mask)

    pack(acc, own[0])
    for d in range(1, reach + 1):

        @pl.when(chip >= d)
        def _():
            for slot in range(2):
                part_copy(d, slot).wait_recv()

    def final(slot, out):
        finish(meta, first + slot, rows, [own[slot]] + list(part_in[slot::2]), out)

    for slot in range(2):

        @pl.when(core == slot)
        def _():
            final(1 - slot, give_away)

    give = pltpu.make_async_remote_copy(
        src_ref=give_away,
        dst_ref=got,
        send_sem=done_sems.at[0],
        recv_sem=done_sems.at[1],
        device_id=at_seq(peer),
        device_id_type=MESH,
    )
    give.start()
    for slot in range(2):

        @pl.when(core == slot)
        def _():
            final(slot, done)

    width = done.shape[1]
    out[:, pl.ds(pl.multiple_of(core * width, HEAD), width)] = done[...]
    give.wait()
    out[:, pl.ds(pl.multiple_of((1 - core) * width, HEAD), width)] = got[...]

    for d in range(1, reach + 1):

        @pl.when(chip >= d)
        def _():
            for slot in range(2):
                q_copy(d, slot).wait_send()

        @pl.when(chip + d < chips)
        def _():
            for slot in range(2):
                part_copy(d, slot).wait_send()

    @pl.when(chip + far < chips)
    def _():
        for copy in tails:
            copy.wait_send()


def body(queries, keys, values, dirty, spans):
    n = lax.axis_size("seq")
    bf = jnp.bfloat16
    shape = jax.ShapeDtypeStruct
    rows, width = keys.shape[0], keys.shape[1] // 2
    q_width = queries.shape[1] // 2
    reach = WINDOW // (2 * rows)
    own = jnp.concatenate([dirty[:, None], spans], axis=1)
    own = jnp.pad(own, ((0, 7), (0, HEAD - 3)))
    meta, q, k, v = pl.pallas_call(
        functools.partial(exchange_kernel, n),
        out_shape=(
            shape((n, 8, HEAD), jnp.int32),
            shape((2 * BLOCK, q_width), bf),
            shape((2 * rows, width), bf),
            shape((2 * rows, width), bf),
        ),
        in_specs=[ANY] * 4,
        out_specs=(ANY,) * 4,
        scratch_shapes=[
            pltpu.SemaphoreType.DMA((2, n)),
            pltpu.SemaphoreType.DMA((2, 3)),
            pltpu.SemaphoreType.DMA((4,)),
        ],
        compiler_params=pltpu.CompilerParams(collective_id=0, has_side_effects=True),
    )(own, queries, keys, values)
    meta = meta[:, 0, :3].reshape(-1)
    part = pltpu.VMEM((BLOCK, q_width + HEAD), bf)
    block = pltpu.VMEM((BLOCK, q_width), bf)
    dma = pltpu.SemaphoreType.DMA
    return pl.pallas_call(
        functools.partial(serve_kernel, n, reach),
        out_shape=shape(queries.shape, bf),
        in_specs=[SMEM, VMEM, VMEM, VMEM],
        out_specs=VMEM,
        scratch_shapes=[
            [block] * 2,
            pltpu.VMEM(k.shape, bf),
            pltpu.VMEM(v.shape, bf),
            pltpu.VMEM((2 * rows, HEAD), bf),
            [block] * (2 * reach),
            [part] * (2 * reach),
            [part] * (2 * reach),
            [part] * 2,
            pltpu.VMEM((BLOCK, width), bf),
            pltpu.VMEM((BLOCK, width), bf),
            pltpu.VMEM((BLOCK, HEAD), bf),
            pltpu.VMEM((width // HEAD, 2 * BLOCK, 2 * HEAD), jnp.float32),
            pltpu.VMEM((BLOCK, q_width), bf),
            pltpu.VMEM((BLOCK, q_width), bf),
            pltpu.VMEM((BLOCK, q_width), bf),
            dma((2, reach, 2)),
            dma((2, reach, 2)),
            dma((2, 3)),
            dma((2,)),
        ],
        compiler_params=pltpu.CompilerParams(
            collective_id=1, has_side_effects=True, vmem_limit_bytes=48 * 1024 * 1024
        ),
    )(meta, q, k, v)


def solution(mesh):
    placed = (
        P(("groups", "seq"), None),
        P(("groups", "seq"), None),
        P(("groups", "seq"), None),
        P(("groups", "seq")),
        P(("groups", "seq"), None),
    )
    return jax.shard_map(
        body, mesh=mesh, in_specs=placed, out_specs=P(("groups", "seq"), None), check_vma=False
    )
```

time: 493 us -> 199 us (0.40); the launches traced: 487 us -> 198 us
  waiting for transfers between devices: 194 us -> 0 us
  Pallas kernels: 0 us -> 191 us
  matrix products: 179 us -> 0 us
  starting transfers between devices: 30.5 us -> 0 us
  blocking collectives: 29.9 us -> 0 us
  other arithmetic: 26.7 us -> 0.73 us
  local copies, waits for them, and re-layouts: 20.1 us -> 5.33 us
  between operations: 5.9 us -> 0.68 us
    ppermute x15 -> x0, waiting for transfers between devices: 194 us -> none  [from_behind(): return lax.ppermute(array, axis, pairs)]
    pallas_call x0 -> x2, Pallas kernels: none -> 191 us  [the longest x1 109 us: body(): pl.pallas_call(functools.partial(serve_kernel, n, reach), out_shape=shape...]
    dot_general x24 -> x0, matrix products: 179 us -> none  [the longest x12 91.1 us: visit(): jnp.einsum('nexi,inv->xnev', weight.astype(jnp.bfloat16), tile_v, preferr...]
    ppermute x15 -> x0, starting transfers between devices: 30.5 us -> none  [from_behind(): return lax.ppermute(array, axis, pairs)]
    all_gather x1 -> x0, blocking collectives: 16.8 us -> none  [body(): lax.all_gather(spans, 'seq', axis=0, tiled=True)]
    unnamed x1 -> x0, blocking collectives: 13.1 us -> none
    convert_element_type x4 -> x0, other arithmetic: 8.12 us -> none  [the longest x1 5.98 us: body(): result.reshape(BLOCK_ROWS, q_heads * HEAD_DIMENSION).astype(jnp.bfloat16)]
    unnamed x17 -> x5, local copies, waits for them, and re-layouts: 11.2 us -> 3.78 us
  transfers between devices with their start and end apart: 15 -> 0, of which waited for: 4 -> 0; matrix products, arithmetic and copies ran while one was open for 43% -> 0% of each run, Pallas kernels for 0% -> 0%
where the time goes in v2:
time: 199 us; the launch traced here: 198 us
  Pallas kernels  191 us (96%)
  local copies, waits for them, and re-layouts  5.33 us (3%)
    pallas_call x1, Pallas kernels, body(): pl.pallas_call(functools.partial(serve_kernel, n, reach), out_shape=shape...  109 us
    pallas_call x1, Pallas kernels, body(): pl.pallas_call(functools.partial(exchange_kernel, n), out_shape=(shape((n...  82.7 us

profile of v2, /device:TPU:28, one launch (start us, length us, event | category | flops | bytes accessed | tf_op | source)
XLA Modules:
  0.0 198.0 jit_solution(6011674820352270799)
XLA Ops:
  0.7 0.7 pad_add_fusion
  1.4 0.6 pad.4.own
  2.0 82.7 %shard_map.55 = (s32[16,8,128]{2,1,0:T(8,128)}, bf16[512,1024]{1,0:T(8,128)(2,1)}, bf16[2048,512]{1,0:T(8,128)(2,1)}, bf16[2048,512]{1,0:T(8,128)(2,1)}) custom-call(s32[8,128]{1,0:T(8,128)} %pad.4.own, bf16[256,2048]{1,0:T(8,128)(2,1)} %q.1, bf16[1024,1024]{1,0:T(8,128)(2,1)} %k.1, bf16[1024,1024]{1,0:T(8,128)(2,1)} %v.1), custom_call_target="tpu_custom_call" | custom-call | tf_op jit(solution)/shard_map/pallas_call | solution.py:469
  84.7 0.9 slice_reduce_fusion
  85.5 0.1 reshape_squeeze.3.meta
  85.6 0.0 copy-start
  85.6 1.6 copy-done
  87.2 0.0 copy-start.1
  87.2 1.2 copy-done.1
  88.4 108.6 %shard_map.56 = bf16[256,2048]{1,0:T(8,128)(2,1)S(1)} custom-call(s32[48]{0:T(128)S(1)} %reshape_squeeze.3.meta, bf16[512,1024]{1,0:T(8,128)(2,1)S(1)} %copy-done.1, bf16[2048,512]{1,0:T(8,128)(2,1)S(1)} %copy-done, bf16[2048,512]{1,0:T(8,128)(2,1)} %get-tuple-element.12.v_raw), custom_call_target="tpu_custom_call" | custom-call | tf_op jit(solution)/shard_map/pallas_call | solution.py:490
  197.0 1.0 copy.8
Async XLA Ops:
  85.6 1.6 copy-start
  87.2 1.2 copy-start.1

commit v3 on v2

--- a/solution.py
+++ b/solution.py
@@ -65,10 +65,8 @@
     pl.semaphore_wait(barrier, count)
 
 
-def exchange_kernel(n, own, q, k, v, meta, q_all, k_all, v_all, meta_sems, sems, local_sems):
+def exchange_kernel(n, own, meta, meta_sems, local_sem):
     me = lax.axis_index("seq")
-    core = lax.rem(me, 2)
-    peer = me + 1 - 2 * core
     barrier = pltpu.get_barrier_semaphore()
 
     @pl.loop(1, n)
@@ -92,28 +90,9 @@
     def _(i):
         meta_copy(i, me, lax.rem(me + i, n)).start()
 
-    copies = []
-    for index, (source, target) in enumerate(((q, q_all), (k, k_all), (v, v_all))):
-        rows, width = source.shape[0], source.shape[1] // 2
-        theirs = pl.ds(pl.multiple_of((1 - core) * width, HEAD), width)
-        mine = pl.ds(pl.multiple_of(core * width, HEAD), width)
-        to = pl.ds(pl.multiple_of(core * rows, BLOCK), rows)
-        remote = pltpu.make_async_remote_copy(
-            src_ref=source.at[:, theirs],
-            dst_ref=target.at[to, :],
-            send_sem=sems.at[0, index],
-            recv_sem=sems.at[1, index],
-            device_id=at_seq(peer),
-            device_id_type=MESH,
-        )
-        remote.start()
-        local = pltpu.make_async_copy(source.at[:, mine], target.at[to, :], local_sems.at[index])
-        local.start()
-        copies += [remote, local]
-    local = pltpu.make_async_copy(own, meta.at[me], local_sems.at[3])
+    local = pltpu.make_async_copy(own, meta.at[me], local_sem)
     local.start()
-    for copy in copies + [local]:
-        copy.wait()
+    local.wait()
 
     @pl.loop(1, n)
     def _(i):
@@ -122,7 +101,7 @@
         meta_copy(i, sender, sender).wait_recv()
 
 
-def rope_q(meta, shard, slot, raw_rows, source, out):
+def rope_q(meta, shard, raw_rows, source, out):
     half = BLOCK // 2
     block = jnp.maximum(meta[3 * shard], 0)
     begin = meta[3 * shard + 1]
@@ -139,16 +118,15 @@
         row = row + jnp.where(lane < HEAD // 2, 0, half)
         both = tables(row, base, begin, length)
         for part in range(2):
-            rows = pl.ds(pl.multiple_of(slot * BLOCK + at + part * half, tile), tile)
             here = pl.ds(pl.multiple_of(at + part * half, tile), tile)
             for h in range(out.shape[1] // HEAD):
                 cols = pl.ds(h * HEAD, HEAD)
-                x = rotate(source[rows, cols], both[part]) * QUERY_SCALE
+                x = rotate(source[here, cols], both[part]) * QUERY_SCALE
                 out[here, cols] = x.astype(jnp.bfloat16)
 
 
 def prepare(meta, shard, slot, k_ref, v_ref, k_out, v_out, live_out):
-    rows = k_ref.shape[0] // 2
+    rows = k_ref.shape[0]
     half = rows // 2
     begin = meta[3 * shard + 1]
     finish = meta[3 * shard + 2]
@@ -165,15 +143,16 @@
         both = tables(row, base, begin, finish - begin)
         for part in range(2):
             src = at + part * half
+            here = pl.ds(pl.multiple_of(src, tile), tile)
             place = pl.ds(pl.multiple_of(slot * rows + src, tile), tile)
             raw = iota + raw0 + src
             live = jnp.where((raw >= begin) & (raw < finish), 0.0, 1.0)
             live_out[place, :] = live.astype(jnp.bfloat16)
             for h in range(k_out.shape[1] // HEAD):
                 cols = pl.ds(h * HEAD, HEAD)
-                x = rotate(k_ref[place, cols], both[part])
+                x = rotate(k_ref[here, cols], both[part])
                 k_out[place, cols] = x.astype(jnp.bfloat16)
-                y = v_ref[place, cols].astype(jnp.float32) * live
+                y = v_ref[here, cols].astype(jnp.float32) * live
                 v_out[place, cols] = y.astype(jnp.bfloat16)
 
 
@@ -258,7 +237,7 @@
 
 
 def serve_kernel(
-    n, reach, meta, q_raw, k_raw, v_raw, out,
+    n, reach, meta, q_mine, q_other, k_mine, k_other, v_mine, v_other, out,
     q, k, v, live, q_in, part_out, part_in, own, tail_k, tail_v, tail_live, acc, done, give_away, got,
     q_sems, part_sems, tail_sems, done_sems,
 ):
@@ -311,12 +290,37 @@
         for i, (source, target) in enumerate(((k, tail_k), (v, tail_v), (live, tail_live)))
     ]
 
+    def forward(slot):
+        return pltpu.make_async_remote_copy(
+            src_ref=q_in[2 + slot],
+            dst_ref=q_in[slot],
+            send_sem=q_sems.at[0, 0, slot],
+            recv_sem=q_sems.at[1, 0, slot],
+            device_id=at_seq(jnp.minimum(me + 2, n - 2 + core)),
+            device_id_type=MESH,
+        )
+
+    odd = lax.rem(chip, 2) == 1
+    passes_on = jnp.logical_not(odd) & (chip + 2 < chips)
+
+    def pass_on(slot):
+        @pl.when(passes_on)
+        def _():
+            q_copy(2, slot).wait_recv()
+            forward(slot).start()
+
     for slot in range(2):
-        rope_q(meta, first + slot, slot, rows, q_raw, q[slot])
+        for side in range(2):
+
+            @pl.when(core == side)
+            def _():
+                source = q_mine if side == slot else q_other
+                rope_q(meta, first + slot, rows, source, q[slot])
+
     for slot in range(2):
-        for d in range(1, reach + 1):
-
-            @pl.when(chip >= d)
+        for d in range(reach, 0, -1):
+
+            @pl.when((chip >= d) & odd if d == 1 else chip >= d)
             def _():
                 q_copy(d, slot).start()
 
@@ -327,10 +331,9 @@
             for ref in part_in[2 * d - 2 : 2 * d]:
                 ref[...] = jnp.zeros_like(ref)
 
-    @pl.loop(0, 2)
-    def _(i):
-        slot = 1 - i
-        prepare(meta, first + slot, slot, k_raw, v_raw, k, v, live)
+    prepare(meta, me, core, k_mine, v_mine, k, v, live)
+    prepare(meta, peer, 1 - core, k_other, v_other, k, v, live)
+    pass_on(0)
 
     @pl.when(chip + far < chips)
     def _():
@@ -359,14 +362,22 @@
 
     own_part(1)
     pack(acc, own[1])
-
-    for d in range(1, reach + 1):
+    pass_on(1)
+
+    for d in range(reach, 0, -1):
 
         @pl.when(chip + d < chips)
         def _():
             for slot in range(2):
                 source = q_in[2 * d - 2 + slot]
-                q_copy(d, slot).wait_recv()
+                if d == 2:
+
+                    @pl.when(jnp.logical_not(passes_on))
+                    def _():
+                        q_copy(d, slot).wait_recv()
+
+                else:
+                    q_copy(d, slot).wait_recv()
                 acc[...] = jnp.zeros_like(acc)
                 if d < reach:
 
@@ -441,7 +452,7 @@
 
     for d in range(1, reach + 1):
 
-        @pl.when(chip >= d)
+        @pl.when((chip >= d) & odd if d == 1 else chip >= d)
         def _():
             for slot in range(2):
                 q_copy(d, slot).wait_send()
@@ -450,6 +461,11 @@
         def _():
             for slot in range(2):
                 part_copy(d, slot).wait_send()
+
+    @pl.when(passes_on)
+    def _():
+        for slot in range(2):
+            forward(slot).wait_send()
 
     @pl.when(chip + far < chips)
     def _():
@@ -464,25 +480,24 @@
     rows, width = keys.shape[0], keys.shape[1] // 2
     q_width = queries.shape[1] // 2
     reach = WINDOW // (2 * rows)
+    core = lax.axis_index("seq") % 2
+    pairs = [(i, i ^ 1) for i in range(n)]
+    halves = []
+    for array in (queries, keys, values):
+        half = array.shape[1] // 2
+        low, high = array[:, :half], array[:, half:]
+        mine = jnp.where(core == 0, low, high)
+        halves += [mine, lax.ppermute(jnp.where(core == 0, high, low), "seq", pairs)]
     own = jnp.concatenate([dirty[:, None], spans], axis=1)
     own = jnp.pad(own, ((0, 7), (0, HEAD - 3)))
-    meta, q, k, v = pl.pallas_call(
+    meta = pl.pallas_call(
         functools.partial(exchange_kernel, n),
-        out_shape=(
-            shape((n, 8, HEAD), jnp.int32),
-            shape((2 * BLOCK, q_width), bf),
-            shape((2 * rows, width), bf),
-            shape((2 * rows, width), bf),
-        ),
-        in_specs=[ANY] * 4,
-        out_specs=(ANY,) * 4,
-        scratch_shapes=[
-            pltpu.SemaphoreType.DMA((2, n)),
-            pltpu.SemaphoreType.DMA((2, 3)),
-            pltpu.SemaphoreType.DMA((4,)),
-        ],
+        out_shape=shape((n, 8, HEAD), jnp.int32),
+        in_specs=[VMEM],
+        out_specs=VMEM,
+        scratch_shapes=[pltpu.SemaphoreType.DMA((2, n)), pltpu.SemaphoreType.DMA],
         compiler_params=pltpu.CompilerParams(collective_id=0, has_side_effects=True),
-    )(own, queries, keys, values)
+    )(own)
     meta = meta[:, 0, :3].reshape(-1)
     part = pltpu.VMEM((BLOCK, q_width + HEAD), bf)
     block = pltpu.VMEM((BLOCK, q_width), bf)
@@ -490,12 +505,12 @@
     return pl.pallas_call(
         functools.partial(serve_kernel, n, reach),
         out_shape=shape(queries.shape, bf),
-        in_specs=[SMEM, VMEM, VMEM, VMEM],
+        in_specs=[SMEM] + [VMEM] * 6,
         out_specs=VMEM,
         scratch_shapes=[
             [block] * 2,
-            pltpu.VMEM(k.shape, bf),
-            pltpu.VMEM(v.shape, bf),
+            pltpu.VMEM((2 * rows, width), bf),
+            pltpu.VMEM((2 * rows, width), bf),
             pltpu.VMEM((2 * rows, HEAD), bf),
             [block] * (2 * reach),
             [part] * (2 * reach),
@@ -516,7 +531,7 @@
         compiler_params=pltpu.CompilerParams(
             collective_id=1, has_side_effects=True, vmem_limit_bytes=48 * 1024 * 1024
         ),
-    )(meta, q, k, v)
+    )(meta, *halves)
 
 
 def solution(mesh):

time: 199 us -> 111 us (0.56)
  Pallas kernels: 191 us -> 101 us
  other arithmetic: 0.73 us -> 4.88 us
  local copies, waits for them, and re-layouts: 5.33 us -> 2.53 us
    pallas_call x1, Pallas kernels: 82.7 us -> 8.41 us  [body(): pl.pallas_call(functools.partial(exchange_kernel, n), out_shape=shape((n,...]
    pallas_call x1, Pallas kernels: 109 us -> 92.7 us  [body(): pl.pallas_call(functools.partial(serve_kernel, n, reach), out_shape=shape...]
    select_n x0 -> x3, other arithmetic: none -> 4.8 us  [body(): jnp.where(core == 0, high, low)]
    unnamed x5 -> x7, local copies, waits for them, and re-layouts: 3.78 us -> 0.98 us
  transfers between devices with their start and end apart: 0 -> 3, of which waited for: 0 -> 0; matrix products, arithmetic and copies ran while one was open for 0% -> 3% of each run, Pallas kernels for 0% -> 8%
where the time goes in v3:
time: 111 us; the launch traced here: 110 us
  Pallas kernels  101 us (91%)
  other arithmetic  4.88 us (4%)
  local copies, waits for them, and re-layouts  2.53 us (2%)
    pallas_call x1, Pallas kernels, body(): pl.pallas_call(functools.partial(serve_kernel, n, reach), out_shape=shape...  92.7 us
    pallas_call x1, Pallas kernels, body(): pl.pallas_call(functools.partial(exchange_kernel, n), out_shape=shape((n,...  8.41 us
    select_n x3, other arithmetic, body(): jnp.where(core == 0, high, low)  4.8 us
  transfers between devices with their start and end apart: 3, of which 0 were waited for; matrix products, arithmetic and copies ran while one was open for 3% of the time, Pallas kernels for 8%

profile of v3, /device:TPU:28, one launch (start us, length us, event | category | flops | bytes accessed | tf_op | source)
XLA Modules:
  0.0 109.7 jit_solution(4420944472069783559)
XLA Ops:
  0.0 0.0 copy-start
  0.0 2.8 %broadcast_select_fusion.2 = (bf16[1024,512]{1,0:T(8,128)(2,1)}, bf16[1024,512]{1,0:T(8,128)(2,1)S(1)}) fusion(pred[]{:T(512)S(6)} %eq.4, bf16[1024,1024]{1,0:T(8,128)(2,1)} %param.6), kind=kLoop, calls=%fused_computation.2 | loop fusion | flops 1048576 | bytes 4194305 | tf_op jit(solution)/shard_map/jit(_where)/select_n | solution.py:490
  2.8 0.0 copy-start.1
  2.8 0.0 collective-permute-start.1
  2.8 0.0 copy-done
  2.8 1.1 %broadcast_select_fusion = (bf16[1024,512]{1,0:T(8,128)(2,1)}, bf16[1024,512]{1,0:T(8,128)(2,1)S(1)}) fusion(pred[]{:T(512)S(6)} %eq.4, bf16[1024,1024]{1,0:T(8,128)(2,1)S(1)} %copy-done), kind=kLoop, calls=%fused_computation | loop fusion | flops 1048576 | bytes 4194305 | tf_op jit(solution)/shard_map/jit(_where)/select_n | solution.py:490
  4.0 0.0 copy-start.2
  4.0 0.5 collective-permute-start.2
  4.5 0.0 copy-done.1
  4.5 0.9 broadcast_select_fusion.4
  5.3 0.0 collective-permute-start
  6.0 0.0 copy-done.2
  6.0 0.1 pad_add_fusion
  6.1 0.6 pad.4.own
  6.7 8.4 %shard_map.55 = s32[16,8,128]{2,1,0:T(8,128)} custom-call(s32[8,128]{1,0:T(8,128)} %pad.4.own), custom_call_target="tpu_custom_call" | custom-call | tf_op jit(solution)/shard_map/pallas_call | solution.py:493
  15.1 0.9 slice_reduce_fusion
  15.9 0.1 reshape_squeeze.3.meta
  16.0 0.0 collective-permute-done.q_other
  16.0 0.0 collective-permute-done.1.k_other
  16.1 0.0 collective-permute-done.2.v_other
  16.1 92.7 %shard_map.56 = bf16[256,2048]{1,0:T(8,128)(2,1)S(1)} custom-call(s32[48]{0:T(128)S(1)} %reshape_squeeze.3.meta, bf16[256,1024]{1,0:T(8,128)(2,1)S(1)} %get-tuple-element.10.q_mine, bf16[256,1024]{1,0:T(8,128)(2,1)S(1)} %collective-permute-done.q_other, bf16[1024,512]{1,0:T(8,128)(2,1)S(1)} %get-tuple-element.8.k_mine, ...), custom_call_target="tpu_custom_call" | custom-call | tf_op jit(solution)/shard_map/pallas_call | solution.py:505
  108.8 1.0 copy.8
Async XLA Ops:
  0.0 2.8 %copy-start = (bf16[1024,1024]{1,0:T(8,128)(2,1)S(1)}, bf16[1024,1024]{1,0:T(8,128)(2,1)}, u32[]{:S(2)}) copy-start(bf16[1024,1024]{1,0:T(8,128)(2,1)} %param.7) | copy-start | bytes 6291460
  2.8 1.7 %copy-start.1 = (bf16[256,2048]{1,0:T(8,128)(2,1)S(1)}, bf16[256,2048]{1,0:T(8,128)(2,1)}, u32[]{:S(2)}) copy-start(bf16[256,2048]{1,0:T(8,128)(2,1)} %param.5) | copy-start | bytes 3145732
  2.8 13.2 %collective-permute-start.1 = (bf16[1024,512]{1,0:T(8,128)(2,1)}, bf16[1024,512]{1,0:T(8,128)(2,1)}, u32[]{:S(2)}, u32[]{:S(2)}) collective-permute-start(bf16[1024,512]{1,0:T(8,128)(2,1)} %get-tuple-element.7), channel_id=1, source_target_pairs={{0,1},{1,0},{2,3},{3,2},{4,5},{5,4},{6,7},{7,6},{8,9},{9,8},{10,11... | collective-permute-start | bytes 3145736 | tf_op jit(solution)/shard_map/ppermute | solution.py:490
  4.0 2.0 %copy-start.2 = (s32[1,2]{1,0:T(1,128)S(1)}, s32[1,2]{1,0:T(1,128)}, u32[]{:S(2)}) copy-start(s32[1,2]{1,0:T(1,128)} %param.9) | copy-start | bytes 28
  4.0 12.1 %collective-permute-start.2 = (bf16[1024,512]{1,0:T(8,128)(2,1)}, bf16[1024,512]{1,0:T(8,128)(2,1)}, u32[]{:S(2)}, u32[]{:S(2)}) collective-permute-start(bf16[1024,512]{1,0:T(8,128)(2,1)} %get-tuple-element.5), channel_id=1, source_target_pairs={{0,1},{1,0},{2,3},{3,2},{4,5},{5,4},{6,7},{7,6},{8,9},{9,8},{10,11... | collective-permute-start | bytes 3145736 | tf_op jit(solution)/shard_map/ppermute | solution.py:490
  5.3 10.7 %collective-permute-start = (bf16[256,1024]{1,0:T(8,128)(2,1)}, bf16[256,1024]{1,0:T(8,128)(2,1)S(1)}, u32[]{:S(2)}, u32[]{:S(2)}) collective-permute-start(bf16[256,1024]{1,0:T(8,128)(2,1)} %get-tuple-element.9), channel_id=1, source_target_pairs={{0,1},{1,0},{2,3},{3,2},{4,5},{5,4},{6,7},{7,6},{8,9},{9,8},{10,11... | collective-permute-start | bytes 1572872 | tf_op jit(solution)/shard_map/ppermute | solution.py:490

commit v4 on v3

--- a/solution.py
+++ b/solution.py
@@ -11,6 +11,7 @@
 HEAD = 128
 WINDOW = 4096
 BLOCK = 256
+TILE = 32
 CAP = 50.0
 QUERY_SCALE = 144.0 ** (-0.5)
 LOG2E = math.log2(math.e)
@@ -27,20 +28,33 @@
     return lax.fori_loop(0, shard, add, jnp.int32(0))
 
 
-def tables(row, base, begin, length):
-    lane = lax.broadcasted_iota(jnp.int32, row.shape, 1)
+def frequency(shape):
+    lane = lax.broadcasted_iota(jnp.int32, shape, 1)
     order = (lane % (HEAD // 2)).astype(jnp.float32)
-    freq = jnp.exp(order * (-2.0 * math.log(10000.0) / HEAD))
-    place = row - base - jnp.clip(row - begin, 0, length)
-    angle = place.astype(jnp.float32) * freq
-    low = lane < HEAD // 2
+    return jnp.exp(order * (-2.0 * math.log(10000.0) / HEAD))
+
+
+def row_tables():
+    row = lax.broadcasted_iota(jnp.int32, (TILE, HEAD), 0)
+    angle = row.astype(jnp.float32) * frequency(row.shape)
+    return jnp.cos(angle), jnp.sin(angle)
+
+
+def tables(start, base, begin, length, small):
+    which = lax.broadcasted_iota(jnp.int32, (8, HEAD), 0)
+    place = start - base + (which // 2) * TILE - jnp.where(which % 2 == 1, length, 0)
+    angle = place.astype(jnp.float32) * frequency(which.shape)
     cosine, sine = jnp.cos(angle), jnp.sin(angle)
-    cosine_swap = pltpu.roll(cosine, HEAD // 2, 1)
-    sine_swap = pltpu.roll(sine, HEAD // 2, 1)
-    return (
-        (jnp.where(low, cosine, cosine_swap), jnp.where(low, -sine, sine_swap)),
-        (jnp.where(low, cosine_swap, cosine), jnp.where(low, -sine_swap, sine)),
-    )
+    row = lax.broadcasted_iota(jnp.int32, (TILE, HEAD), 0)
+    low = lax.broadcasted_iota(jnp.int32, (TILE, HEAD), 1) < HEAD // 2
+    result = []
+    for t in range(4):
+        after = row + (start + t * TILE) >= begin
+        c = jnp.where(after, cosine[2 * t + 1 : 2 * t + 2], cosine[2 * t : 2 * t + 1])
+        s = jnp.where(after, sine[2 * t + 1 : 2 * t + 2], sine[2 * t : 2 * t + 1])
+        turned = s * small[0] + c * small[1]
+        result.append((c * small[0] - s * small[1], jnp.where(low, -turned, turned)))
+    return result
 
 
 def rotate(x, table):
@@ -101,57 +115,46 @@
         meta_copy(i, sender, sender).wait_recv()
 
 
-def rope_q(meta, shard, raw_rows, source, out):
-    half = BLOCK // 2
+def rope_q(meta, shard, raw_rows, source, out, small):
     block = jnp.maximum(meta[3 * shard], 0)
     begin = meta[3 * shard + 1]
     length = meta[3 * shard + 2] - begin
     base = removed_before(meta, shard)
     raw0 = shard * raw_rows + block * BLOCK
-    tile = 32
-
-    @pl.loop(0, half // tile)
+
+    @pl.loop(0, BLOCK // (4 * TILE))
     def _(step):
-        at = step * tile
-        row = lax.broadcasted_iota(jnp.int32, (tile, HEAD), 0) + raw0 + at
-        lane = lax.broadcasted_iota(jnp.int32, (tile, HEAD), 1)
-        row = row + jnp.where(lane < HEAD // 2, 0, half)
-        both = tables(row, base, begin, length)
-        for part in range(2):
-            here = pl.ds(pl.multiple_of(at + part * half, tile), tile)
+        at = step * (4 * TILE)
+        for part, table in enumerate(tables(raw0 + at, base, begin, length, small)):
+            here = pl.ds(pl.multiple_of(at + part * TILE, TILE), TILE)
             for h in range(out.shape[1] // HEAD):
                 cols = pl.ds(h * HEAD, HEAD)
-                x = rotate(source[here, cols], both[part]) * QUERY_SCALE
+                x = rotate(source[here, cols], table) * QUERY_SCALE
                 out[here, cols] = x.astype(jnp.bfloat16)
 
 
-def prepare(meta, shard, slot, k_ref, v_ref, k_out, v_out, live_out):
+def prepare(meta, shard, slot, k_ref, v_ref, k_out, v_out, live_out, small):
     rows = k_ref.shape[0]
-    half = rows // 2
     begin = meta[3 * shard + 1]
     finish = meta[3 * shard + 2]
     base = removed_before(meta, shard)
     raw0 = shard * rows
-    tile = 32
-
-    @pl.loop(0, half // tile)
+
+    @pl.loop(0, rows // (4 * TILE))
     def _(step):
-        at = step * tile
-        iota = lax.broadcasted_iota(jnp.int32, (tile, HEAD), 0)
-        lane = lax.broadcasted_iota(jnp.int32, (tile, HEAD), 1)
-        row = iota + raw0 + at + jnp.where(lane < HEAD // 2, 0, half)
-        both = tables(row, base, begin, finish - begin)
-        for part in range(2):
-            src = at + part * half
-            here = pl.ds(pl.multiple_of(src, tile), tile)
-            place = pl.ds(pl.multiple_of(slot * rows + src, tile), tile)
+        at = step * (4 * TILE)
+        iota = lax.broadcasted_iota(jnp.int32, (TILE, HEAD), 0)
+        turns = tables(raw0 + at, base, begin, finish - begin, small)
+        for part, table in enumerate(turns):
+            src = at + part * TILE
+            here = pl.ds(pl.multiple_of(src, TILE), TILE)
+            place = pl.ds(pl.multiple_of(slot * rows + src, TILE), TILE)
             raw = iota + raw0 + src
             live = jnp.where((raw >= begin) & (raw < finish), 0.0, 1.0)
             live_out[place, :] = live.astype(jnp.bfloat16)
             for h in range(k_out.shape[1] // HEAD):
                 cols = pl.ds(h * HEAD, HEAD)
-                x = rotate(k_ref[here, cols], both[part])
-                k_out[place, cols] = x.astype(jnp.bfloat16)
+                k_out[place, cols] = rotate(k_ref[here, cols], table).astype(jnp.bfloat16)
                 y = v_ref[here, cols].astype(jnp.float32) * live
                 v_out[place, cols] = y.astype(jnp.bfloat16)
 
@@ -309,13 +312,14 @@
             q_copy(2, slot).wait_recv()
             forward(slot).start()
 
+    small = row_tables()
     for slot in range(2):
         for side in range(2):
 
             @pl.when(core == side)
             def _():
                 source = q_mine if side == slot else q_other
-                rope_q(meta, first + slot, rows, source, q[slot])
+                rope_q(meta, first + slot, rows, source, q[slot], small)
 
     for slot in range(2):
         for d in range(reach, 0, -1):
@@ -331,8 +335,8 @@
             for ref in part_in[2 * d - 2 : 2 * d]:
                 ref[...] = jnp.zeros_like(ref)
 
-    prepare(meta, me, core, k_mine, v_mine, k, v, live)
-    prepare(meta, peer, 1 - core, k_other, v_other, k, v, live)
+    prepare(meta, me, core, k_mine, v_mine, k, v, live, small)
+    prepare(meta, peer, 1 - core, k_other, v_other, k, v, live, small)
     pass_on(0)
 
     @pl.when(chip + far < chips)

time: 111 us -> 106 us (0.955)
  Pallas kernels: 101 us -> 96.8 us
    pallas_call x1, Pallas kernels: 92.7 us -> 88.4 us  [body(): pl.pallas_call(functools.partial(serve_kernel, n, reach), out_shape=shape...]
where the time goes in v4:
time: 106 us; the launch traced here: 105 us
  Pallas kernels  96.8 us (91%)
  other arithmetic  4.88 us (5%)
  local copies, waits for them, and re-layouts  2.53 us (2%)
    pallas_call x1, Pallas kernels, body(): pl.pallas_call(functools.partial(serve_kernel, n, reach), out_shape=shape...  88.4 us
    pallas_call x1, Pallas kernels, body(): pl.pallas_call(functools.partial(exchange_kernel, n), out_shape=shape((n,...  8.41 us
    select_n x3, other arithmetic, body(): jnp.where(core == 0, high, low)  4.8 us
  transfers between devices with their start and end apart: 3, of which 0 were waited for; matrix products, arithmetic and copies ran while one was open for 3% of the time, Pallas kernels for 8%

profile of v4, /device:TPU:28, one launch (start us, length us, event | category | flops | bytes accessed | tf_op | source)
XLA Modules:
  0.0 105.5 jit_solution(1590364834458598989)
XLA Ops:
  0.0 0.0 copy-start
  0.0 2.8 %broadcast_select_fusion.2 = (bf16[1024,512]{1,0:T(8,128)(2,1)}, bf16[1024,512]{1,0:T(8,128)(2,1)S(1)}) fusion(pred[]{:T(512)S(6)} %eq.4, bf16[1024,1024]{1,0:T(8,128)(2,1)} %param.6), kind=kLoop, calls=%fused_computation.2 | loop fusion | flops 1048576 | bytes 4194305 | tf_op jit(solution)/shard_map/jit(_where)/select_n | solution.py:494
  2.8 0.0 copy-start.1
  2.8 0.0 collective-permute-start.1
  2.8 0.0 copy-done
  2.8 1.1 %broadcast_select_fusion = (bf16[1024,512]{1,0:T(8,128)(2,1)}, bf16[1024,512]{1,0:T(8,128)(2,1)S(1)}) fusion(pred[]{:T(512)S(6)} %eq.4, bf16[1024,1024]{1,0:T(8,128)(2,1)S(1)} %copy-done), kind=kLoop, calls=%fused_computation | loop fusion | flops 1048576 | bytes 4194305 | tf_op jit(solution)/shard_map/jit(_where)/select_n | solution.py:494
  4.0 0.0 copy-start.2
  4.0 0.5 collective-permute-start.2
  4.5 0.0 copy-done.1
  4.5 0.9 broadcast_select_fusion.4
  5.3 0.0 collective-permute-start
  6.0 0.0 copy-done.2
  6.0 0.1 pad_add_fusion
  6.1 0.6 pad.4.own
  6.7 8.4 %shard_map.55 = s32[16,8,128]{2,1,0:T(8,128)} custom-call(s32[8,128]{1,0:T(8,128)} %pad.4.own), custom_call_target="tpu_custom_call" | custom-call | tf_op jit(solution)/shard_map/pallas_call | solution.py:497
  15.1 0.9 slice_reduce_fusion
  15.9 0.1 reshape_squeeze.3.meta
  16.0 0.0 collective-permute-done.q_other
  16.0 0.0 collective-permute-done.1.k_other
  16.1 0.0 collective-permute-done.2.v_other
  16.1 88.4 %shard_map.56 = bf16[256,2048]{1,0:T(8,128)(2,1)S(1)} custom-call(s32[48]{0:T(128)S(1)} %reshape_squeeze.3.meta, bf16[256,1024]{1,0:T(8,128)(2,1)S(1)} %get-tuple-element.10.q_mine, bf16[256,1024]{1,0:T(8,128)(2,1)S(1)} %collective-permute-done.q_other, bf16[1024,512]{1,0:T(8,128)(2,1)S(1)} %get-tuple-element.8.k_mine, ...), custom_call_target="tpu_custom_call" | custom-call | tf_op jit(solution)/shard_map/pallas_call | solution.py:509
  104.5 1.0 copy.8
Async XLA Ops:
  0.0 2.8 %copy-start = (bf16[1024,1024]{1,0:T(8,128)(2,1)S(1)}, bf16[1024,1024]{1,0:T(8,128)(2,1)}, u32[]{:S(2)}) copy-start(bf16[1024,1024]{1,0:T(8,128)(2,1)} %param.7) | copy-start | bytes 6291460
  2.8 1.7 %copy-start.1 = (bf16[256,2048]{1,0:T(8,128)(2,1)S(1)}, bf16[256,2048]{1,0:T(8,128)(2,1)}, u32[]{:S(2)}) copy-start(bf16[256,2048]{1,0:T(8,128)(2,1)} %param.5) | copy-start | bytes 3145732
  2.8 13.2 %collective-permute-start.1 = (bf16[1024,512]{1,0:T(8,128)(2,1)}, bf16[1024,512]{1,0:T(8,128)(2,1)}, u32[]{:S(2)}, u32[]{:S(2)}) collective-permute-start(bf16[1024,512]{1,0:T(8,128)(2,1)} %get-tuple-element.7), channel_id=1, source_target_pairs={{0,1},{1,0},{2,3},{3,2},{4,5},{5,4},{6,7},{7,6},{8,9},{9,8},{10,11... | collective-permute-start | bytes 3145736 | tf_op jit(solution)/shard_map/ppermute | solution.py:494
  4.0 2.0 %copy-start.2 = (s32[1,2]{1,0:T(1,128)S(1)}, s32[1,2]{1,0:T(1,128)}, u32[]{:S(2)}) copy-start(s32[1,2]{1,0:T(1,128)} %param.9) | copy-start | bytes 28
  4.0 12.1 %collective-permute-start.2 = (bf16[1024,512]{1,0:T(8,128)(2,1)}, bf16[1024,512]{1,0:T(8,128)(2,1)}, u32[]{:S(2)}, u32[]{:S(2)}) collective-permute-start(bf16[1024,512]{1,0:T(8,128)(2,1)} %get-tuple-element.5), channel_id=1, source_target_pairs={{0,1},{1,0},{2,3},{3,2},{4,5},{5,4},{6,7},{7,6},{8,9},{9,8},{10,11... | collective-permute-start | bytes 3145736 | tf_op jit(solution)/shard_map/ppermute | solution.py:494
  5.3 10.7 %collective-permute-start = (bf16[256,1024]{1,0:T(8,128)(2,1)}, bf16[256,1024]{1,0:T(8,128)(2,1)S(1)}, u32[]{:S(2)}, u32[]{:S(2)}) collective-permute-start(bf16[256,1024]{1,0:T(8,128)(2,1)} %get-tuple-element.9), channel_id=1, source_target_pairs={{0,1},{1,0},{2,3},{3,2},{4,5},{5,4},{6,7},{7,6},{8,9},{9,8},{10,11... | collective-permute-start | bytes 1572872 | tf_op jit(solution)/shard_map/ppermute | solution.py:494
